TPU v7x, 512 devices: a whole 4x4x16 slice. The times are simulated.
512 devices in a mesh: dp: 64 (over z_lo, y, x), mp: 8 (over z_hi, core).
Axes of the slice: x: 4, y: 4, z: 16 (z_hi: 4, z_lo: 4; z = z_hi * 4 + z_lo), core: 2. Of those that a mesh axis runs over, the one named last changes fastest.
Arguments:
- grads: bfloat16 [64, 16, 512, 512], P('dp', 'mp')
- prev_roots: bfloat16 [16, 2, 512, 512], P('mp')
- damping: float32 [4], replicated, may hold values from 0.05 to 1
- block_layer: int32 [16], P('mp'), may hold values from 0 to 3
- owners: int32 [16, 2], P('mp'), may hold values from -1 to 63, as said below
Outputs:
- preconditioned: bfloat16 [64, 16, 512, 512], P('dp', 'mp')
Inputs may be any that keep to these rules, and one draw needn't show every extreme that they name: For each index of mp exactly 2 of its 4 statistics are refreshed (owner >= 0). The owners of the refreshed statistics, taken in order of block and side over the whole table, are consecutive numbers modulo 64, so no two are equal.
All inputs are finite; a program needn't handle non-finite values.
Results may differ from a plain program's by a relative error of at most 0.001.
The roundings to bfloat16 on the way count: a program that leaves them out, or rounds other values in their place, can miss the bound.
Values may be sent and summed in bfloat16 or wider, within the bound.
No kernel may reach another device: no remote copies, remote signals or barrier semaphores. Data moves between devices by JAX's collectives and lax.ppermute only.
A program may use at most 64 MiB of HBM per device.

v0:
```python
import jax
import jax.numpy as jnp
from jax import lax
from jax.sharding import PartitionSpec as P

B = 512
NB = 2
ITERS = 3
LAYERS = 4


NORM_EPSILON = 1e-06
HIGHEST_PRECISION = lax.Precision.HIGHEST


def from_root(block, axis, holder):
    block = jnp.where(lax.axis_index(axis) == holder, block, jnp.zeros_like(block))
    return lax.psum(block, axis)


def newton_root(statistic):
    identity = jnp.eye(B, dtype=jnp.float32)
    norm_scale = 5.0 / (2.0 * jnp.sqrt(jnp.sum(statistic * statistic)))
    mat_m = norm_scale * statistic
    mat_h = jnp.sqrt(jnp.sqrt(norm_scale)) * identity
    for iteration in range(ITERS):
        newton_step = 1.25 * identity - 0.25 * mat_m
        mat_h = jnp.dot(
            mat_h, newton_step, precision=HIGHEST_PRECISION, preferred_element_type=jnp.float32
        )
        square = jnp.dot(
            newton_step,
            newton_step,
            precision=HIGHEST_PRECISION,
            preferred_element_type=jnp.float32,
        )
        fourth = jnp.dot(
            square, square, precision=HIGHEST_PRECISION, preferred_element_type=jnp.float32
        )
        mat_m = jnp.dot(
            fourth, mat_m, precision=HIGHEST_PRECISION, preferred_element_type=jnp.float32
        )
    return mat_h


def per_device(grads, prev_roots, damping, block_layer, owners):
    blocks_here = grads[0]
    stat_count = 2 * NB
    flat_owner = owners.reshape(stat_count)
    positions = jnp.arange(stat_count, dtype=jnp.int32)
    ranked = jnp.argsort(jnp.where(flat_owner >= 0, positions, positions + stat_count))
    chosen = ranked[:NB]
    chosen_owner = flat_owner[chosen]
    layer_match = block_layer[:, None] == jnp.arange(LAYERS, dtype=jnp.int32)[None, :]
    block_damp = jnp.sum(jnp.where(layer_match, damping[None, :], 0.0), axis=1)
    chosen_damp = block_damp[chosen // 2]
    shards = lax.axis_size("dp")
    identity = jnp.eye(B, dtype=jnp.float32)
    left_gram = jnp.einsum(
        "bik,bjk->bij", blocks_here, blocks_here, preferred_element_type=jnp.float32
    )
    right_gram = jnp.einsum(
        "bki,bkj->bij", blocks_here, blocks_here, preferred_element_type=jnp.float32
    )
    partial_terms = jnp.stack([left_gram, right_gram], axis=1).reshape(stat_count, B, B)
    summed = lax.psum(partial_terms, "dp")
    gathered = summed[chosen]
    statistics = gathered / (shards * B)
    traces = jnp.trace(statistics, axis1=1, axis2=2) / B
    damped = statistics + (chosen_damp * traces)[:, None, None] * identity
    own_index = lax.axis_index("dp")
    owner_hits = chosen_owner == own_index
    own_slot = jnp.argmax(owner_hits.astype(jnp.int32))
    own_root = lax.cond(
        jnp.any(owner_hits),
        lambda matrix: newton_root(matrix).astype(jnp.bfloat16),
        lambda matrix: jnp.zeros((B, B), jnp.bfloat16),
        damped[own_slot],
    )
    received = []
    for position in range(NB):
        received.append(from_root(own_root, "dp", chosen_owner[position]))
    new_roots = jnp.stack(received)
    root_table = prev_roots.reshape(stat_count, B, B)
    for position in range(NB):
        root_table = root_table.at[chosen[position]].set(new_roots[position])
    root_table = root_table.reshape(NB, 2, B, B)
    half_product = jnp.einsum(
        "bik,bkj->bij", root_table[:, 0], blocks_here, preferred_element_type=jnp.float32
    ).astype(jnp.bfloat16)
    update = jnp.einsum(
        "bik,bkj->bij", half_product, root_table[:, 1], preferred_element_type=jnp.float32
    )
    grad_sq = jnp.sum(jnp.square(blocks_here.astype(jnp.float32)), axis=(1, 2))
    upd_sq = jnp.sum(update * update, axis=(1, 2))
    layer_grad = jnp.sum(jnp.where(layer_match, grad_sq[:, None], 0.0), axis=0)
    layer_upd = jnp.sum(jnp.where(layer_match, upd_sq[:, None], 0.0), axis=0)
    layer_grad, layer_upd = lax.psum((layer_grad, layer_upd), "mp")
    layer_ratio = jnp.sqrt((layer_grad + NORM_EPSILON) / (layer_upd + NORM_EPSILON))
    block_ratio = jnp.sum(jnp.where(layer_match, layer_ratio[None, :], 0.0), axis=1)
    return (update * block_ratio[:, None, None]).astype(jnp.bfloat16)[None]


def solution(mesh):
    return jax.shard_map(
        per_device,
        mesh=mesh,
        in_specs=(
            P("dp", "mp", None, None),
            P("mp", None, None, None),
            P(),
            P("mp"),
            P("mp", None),
        ),
        out_specs=P("dp", "mp", None, None),
        check_vma=False,
    )
```

profile of v0, /device:TPU:1, one launch (start us, length us, event | category | flops | bytes accessed | tf_op | source)
XLA Modules:
  0.0 1545.8 jit_solution(17131887005688257856)
XLA Ops:
  6.5 1.2 copy-done
  7.8 0.8 convolution_bitcast_fusion
  8.5 0.7 convolution_bitcast_fusion.1
  9.3 0.4 pad_maximum_fusion
  9.7 2.4 copy.10
  12.2 0.6 copy-done.7
  12.9 0.7 sort.17
  13.7 0.6 gather_fusion.2
  14.3 0.6 compare_reduce_fusion
  15.6 0.6 fusion.52
  17.5 1.1 fusion.48
  18.6 0.7 fusion.49
  19.3 688.2 %all-reduce.5.cloned.1.call-done = f32[4,512,512]{2,1,0:T(8,128)} async-done(((f32[4,512,512]{2,1,0:T(8,128)}), f32[4,512,512]{2,1,0:T(8,128)}) %all-reduce.5.cloned.1.call-update) | async-done | bytes 4194320 | tf_op jit(solution)/shard_map/psum | solution.py:66
  707.7 0.8 conditional.1
  707.7 0.8 broadcast.122
  708.6 2.2 select_bitcast_fusion
  710.8 0.6 fusion.51
  715.3 0.8 and_reduce_fusion
  716.5 751.1 %all-reduce.7.cloned.1.call-done = (bf16[1,512,512]{2,1,0:T(8,128)(2,1)}, bf16[1,512,512]{2,1,0:T(8,128)(2,1)}) async-done(((bf16[1,512,512]{2,1,0:T(8,128)(2,1)}, bf16[1,512,512]{2,1,0:T(8,128)(2,1)}), (bf16[1,512,512]{2,1,0:T(8,128)(2,1)}, bf16[1,512,512]{2,1,0:T(8,128)(2,1)})) %all-reduce.7.cloned.1.call-update) | async-done | bytes 1048592 | tf_op jit(solution)/shard_map/psum | solution.py:18
  1467.6 1.9 select_dynamic-update-slice_fusion.1
  1469.5 1.9 select_dynamic-update-slice_fusion
  1471.3 2.6 multiply_reduce_fusion.1
  1474.0 61.8 %all-reduce = (f32[4]{0:T(128)S(1)}, f32[4]{0:T(128)S(1)}) all-reduce(f32[4]{0:T(128)S(1)} %get-tuple-element.310, f32[4]{0:T(128)S(1)} %get-tuple-element.309), channel_id=1, replica_groups=mesh['dp'=64,'mp'=8] {'mp'}, use_global_device_ids=true, to_apply=%region_18.19 | all-reduce | flops 8 | bytes 64 | tf_op jit(solution)/shard_map/psum | solution.py:98
  1536.0 2.9 fusion.43
  (29 shorter events, 1.1 us)
Async XLA Ops:
  6.5 1.2 copy-start
  6.5 701.0 %all-reduce.5.cloned.1.call-start = ((), (), s32[]{:S(2)}) async-start(), calls=%async_computation | async-start | bytes 8388608 | tf_op jit(solution)/shard_map/psum | solution.py:66
  12.1 0.7 copy-start.7
  12.1 6.4 copy-start.5
  12.2 695.6 %copy-start.4 = (f32[4]{0:T(128)S(1)}, f32[4]{0:T(128)}, u32[]{:S(2)}) copy-start(f32[4]{0:T(128)} %param.13) | copy-start | bytes 52
  12.2 1455.4 %all-reduce.7.cloned.1.call-start = ((), (), s32[]{:S(2)}) async-start(), calls=%async_computation.1 | async-start | bytes 2097152 | tf_op jit(solution)/shard_map/psum | solution.py:18
  708.6 6.7 copy-start.6
  708.6 759.0 %copy-start.2 = (bf16[2,2,512,512]{3,2,1,0:T(8,128)(2,1)S(1)}, bf16[2,2,512,512]{3,2,1,0:T(8,128)(2,1)}, u32[]{:S(2)}) copy-start(bf16[2,2,512,512]{3,2,1,0:T(8,128)(2,1)} %param.12) | copy-start | bytes 6291460
Sparse Core Ops, SparseCore 0:
  12.3 695.1 all-reduce.4
  711.0 756.5 all-reduce.6
where the time goes:
time: 1550 us
  waiting for transfers between devices  1440 us (93%)
  blocking collectives  61.8 us (4%)
  between operations  19.3 us (1%)
    psum x1, waiting for transfers between devices, from_root(): return lax.psum(block, axis)  751 us
    psum x1, waiting for transfers between devices, per_device(): summed = lax.psum(partial_terms, 'dp')  688 us
    psum x1, blocking collectives, per_device(): layer_grad, layer_upd = lax.psum((layer_grad, layer_upd), 'mp')  61.8 us
  transfers between devices with their start and end apart: 2, of which 2 were waited for; matrix products, arithmetic and copies ran while one was open for 0% of the time, Pallas kernels for 0%

commit v1 on v0

v1 whole, which is shorter than its diff:
```python
import jax
import jax.numpy as jnp
from jax import lax
from jax.sharding import Mesh, PartitionSpec as P

B = 512
NB = 2
ITERS = 3
LAYERS = 4
SHARDS = 64
NORM_EPSILON = 1e-06
HIGHEST = lax.Precision.HIGHEST
PLANE = ("y", "x")
COLUMN = ("h", "c")


def mm(a, b):
    return jnp.dot(a, b, precision=HIGHEST, preferred_element_type=jnp.float32)


def newton_root(statistic):
    identity = jnp.eye(B, dtype=jnp.float32)
    norm_scale = 5.0 / (2.0 * jnp.sqrt(jnp.sum(statistic * statistic)))
    mat_m = norm_scale * statistic
    mat_h = None
    for iteration in range(ITERS):
        step = 1.25 * identity - 0.25 * mat_m
        mat_h = step if mat_h is None else mm(mat_h, step)
        if iteration + 1 < ITERS:
            square = mm(step, step)
            mat_m = mm(mm(square, square), mat_m)
    return (jnp.sqrt(jnp.sqrt(norm_scale)) * mat_h).astype(jnp.bfloat16)


def spread(a, axes, count):
    return lax.all_to_all(jnp.broadcast_to(a[None], (count,) + a.shape), axes, 0, 0)


def per_device(grads, prev_roots, damping, block_layer, owners):
    g = grads[0]
    fresh = owners.reshape(2 * NB) >= 0
    first = jnp.argmax(fresh)
    last = 2 * NB - 1 - jnp.argmax(fresh[::-1])
    layer_match = block_layer[:, None] == jnp.arange(LAYERS, dtype=jnp.int32)[None, :]
    block_damp = jnp.sum(jnp.where(layer_match, damping[None, :], 0.0), axis=1)

    def gram(stat):
        block = g[stat // 2]
        block = jnp.where(stat % 2 == 0, block, block.T)
        return jnp.dot(block, block.T, preferred_element_type=jnp.float32)

    row = lax.broadcasted_iota(jnp.int32, (B, B), 0)
    col = lax.broadcasted_iota(jnp.int32, (B, B), 1)
    gram_a, gram_b = gram(first), gram(last)
    diag_b = jnp.sum(jnp.where(row == col, gram_b, 0.0), axis=0).reshape(4, 128)
    packed = jnp.where(row >= col, gram_a, gram_b).reshape(16, 32 * 4, 128)
    packed = jnp.concatenate([packed, jnp.broadcast_to(jnp.pad(diag_b, ((0, 4), (0, 0)))[None], (16, 8, 128))], axis=1)
    part = jnp.sum(lax.all_to_all(packed, PLANE, 0, 0), axis=0)
    part = jnp.sum(spread(part, "z", 4), axis=0)
    diag_b = part[128:132].reshape(1, B)
    packed = spread(part[:128], PLANE, 16).reshape(B, B)
    flipped = packed.T
    identity = jnp.eye(B, dtype=jnp.float32)

    def root(statistic, stat):
        statistic = statistic / (SHARDS * B)
        damp = block_damp[stat // 2] * jnp.trace(statistic) / B
        return newton_root(statistic + damp * identity)

    root_a = root(jnp.where(row >= col, packed, flipped), first)
    root_b = root(jnp.where(row == col, diag_b, jnp.where(row < col, packed, flipped)), last)

    def table(block, side):
        stat = 2 * block + side
        old = prev_roots[block, side]
        return jnp.where(stat == first, root_a, jnp.where(stat == last, root_b, old))

    left = jnp.stack([table(b, 0) for b in range(NB)])
    right = jnp.stack([table(b, 1) for b in range(NB)])
    half = jnp.einsum("bik,bkj->bij", left, g, preferred_element_type=jnp.float32).astype(jnp.bfloat16)
    update = jnp.einsum("bik,bkj->bij", half, right, preferred_element_type=jnp.float32)
    grad_sq = jnp.sum(jnp.square(g.astype(jnp.float32)), axis=(1, 2))
    upd_sq = jnp.sum(update * update, axis=(1, 2))
    sums = jnp.stack([grad_sq, upd_sq])
    sums = jnp.sum(jnp.where(layer_match[None], sums[:, :, None], 0.0), axis=1)
    sums = jnp.sum(spread(jnp.pad(sums.reshape(1, 2 * LAYERS), ((0, 0), (0, 120))), COLUMN, 8), axis=0)
    sums = sums[0, : 2 * LAYERS].reshape(2, LAYERS)
    layer_ratio = jnp.sqrt((sums[0] + NORM_EPSILON) / (sums[1] + NORM_EPSILON))
    block_ratio = jnp.sum(jnp.where(layer_match, layer_ratio[None, :], 0.0), axis=1)
    return (update * block_ratio[:, None, None]).astype(jnp.bfloat16)[None]


def solution(mesh):
    dp, mp = ("z", "y", "x"), ("h", "c")
    fine = Mesh(mesh.devices.reshape(4, 4, 4, 4, 2), dp + mp)
    return jax.shard_map(
        per_device,
        mesh=fine,
        in_specs=(P(dp, mp, None, None), P(mp, None, None, None), P(), P(mp), P(mp, None)),
        out_specs=P(dp, mp, None, None),
        check_vma=False,
    )
```

time: 1550 us -> 146 us (0.09)
  waiting for transfers between devices: 1440 us -> 9.38 us
  matrix products: 4.1 us -> 43.3 us
    psum x2 -> x0, waiting for transfers between devices: 1440 us -> none  [the longest x1 751 us: from_root(): return lax.psum(block, axis)]
    all_to_all x0 -> x3, blocking collectives: none -> 65.3 us  [the longest x2 41.8 us: spread(): lax.all_to_all(jnp.broadcast_to(a[None], (count,) + a.shape), axes, 0, 0)]
    psum x1 -> x0, blocking collectives: 61.8 us -> none  [per_device(): layer_grad, layer_upd = lax.psum((layer_grad, layer_upd), 'mp')]
    dot_general x3 -> x19, matrix products: 4.1 us -> 43.3 us  [the longest x16 39.3 us: mm(): return jnp.dot(a, b, precision=HIGHEST, preferred_element_type=jnp.float32)]
  transfers between devices with their start and end apart: 2 -> 1, of which waited for: 2 -> 1; matrix products, arithmetic and copies ran while one was open for 0% -> 1% of each run, Pallas kernels for 0% -> 0%
where the time goes in v1:
time: 146 us
  blocking collectives  65.3 us (45%)
  matrix products  43.3 us (30%)
  between operations  10.7 us (7%)
  waiting for transfers between devices  9.38 us (6%)
  other arithmetic  7.7 us (5%)
  local copies, waits for them, and re-layouts  5.35 us (4%)
  starting transfers between devices  3.84 us (3%)
    all_to_all x2, blocking collectives, spread(): lax.all_to_all(jnp.broadcast_to(a[None], (count,) + a.shape), axes, 0, 0)  41.8 us
    dot_general x16, matrix products, mm(): return jnp.dot(a, b, precision=HIGHEST, preferred_element_type=jnp.float32)  39.3 us
    all_to_all x1, blocking collectives, per_device(): part = jnp.sum(lax.all_to_all(packed, PLANE, 0, 0), axis=0)  23.5 us
    all_to_all x1, waiting for transfers between devices, spread(): lax.all_to_all(jnp.broadcast_to(a[None], (count,) + a.shape), axes, 0, 0)  9.38 us
    all_to_all x1, starting transfers between devices, spread(): lax.all_to_all(jnp.broadcast_to(a[None], (count,) + a.shape), axes, 0, 0)  3.84 us
    dot_general x1, matrix products, per_device(): jnp.einsum('bik,bkj->bij', half, right, preferred_element_type=jnp.float32)  3 us
  transfers between devices with their start and end apart: 1, of which 1 were waited for; matrix products, arithmetic and copies ran while one was open for 1% of the time, Pallas kernels for 0%

profile of v1, /device:TPU:1, one launch (start us, length us, event | category | flops | bytes accessed | tf_op | source)
XLA Modules:
  0.0 145.5 jit_solution(2196447655606127112)
XLA Ops:
  8.5 23.5 %all_to_all.20 = f32[16,136,128]{2,1,0:T(8,128)S(1)} all-to-all(f32[16,136,128]{2,1,0:T(8,128)S(1)} %pad_maximum_fusion), channel_id=1, replica_groups=mesh['z'=4,'y'=4,'x'=4,'h'=4,'c'=2] {'y','x'}, dimensions={0} | all-to-all | bytes 2228224 | tf_op jit(solution)/shard_map/all_to_all | solution.py:58
  32.2 12.9 %all_to_all.21 = f32[4,136,128]{2,1,0:T(8,128)S(1)} all-to-all(f32[4,136,128]{2,1,0:T(8,128)S(1)} %broadcast_in_dim.95), channel_id=1, replica_groups=mesh['z'=4,'y'=4,'x'=4,'h'=4,'c'=2] {'z'}, dimensions={0} | all-to-all | bytes 557056 | tf_op jit(solution)/shard_map/all_to_all | solution.py:36
  46.2 3.8 %all-to-all-start.2 = ((f32[16,128,128]{2,1,0:T(8,128)}), f32[16,128,128]{2,1,0:T(8,128)S(1)}, u32[]{:S(2)}, u32[]{:S(2)}) async-start(f32[16,128,128]{2,1,0:T(8,128)} %broadcast_in_dim.96), calls=%async_computation.2 | async-start | bytes 2097152 | tf_op jit(solution)/shard_map/all_to_all | solution.py:36
  54.2 9.4 %all-to-all-done.2 = f32[16,128,128]{2,1,0:T(8,128)S(1)} async-done(((f32[16,128,128]{2,1,0:T(8,128)}), f32[16,128,128]{2,1,0:T(8,128)S(1)}, u32[]{:S(2)}, u32[]{:S(2)}) %all-to-all-start.2) | async-done | bytes 1048608 | tf_op jit(solution)/shard_map/all_to_all | solution.py:36
  65.0 2.2 %select_reduce_fusion = (f32[]{:T(128)}, f32[512,512]{1,0:T(8,128)S(1)}, f32[]{:T(128)}, f32[512,512]{1,0:T(8,128)S(1)}) fusion(f32[512,512]{1,0:T(8,128)S(1)} %reshape.54, f32[512,512]{0,1:T(8,128)} %copy.18, f32[512]{0:T(512)S(1)} %slice_bitcast_fusion), kind=kLoop, calls=%fused_computation.34 | loop fusion | flops 3145726 | bytes 4196360 | tf_op jit(solution)/shard_map/jit(trace)/reduce_sum | solution.py:67
  71.4 2.0 %fusion.26 = f32[512,512]{1,0:T(8,128)S(1)} fusion(f32[]{:T(128)S(6)} %div.47, f32[512,512]{1,0:T(8,128)S(1)} %get-tuple-element.18, f32[]{:T(128)S(6)} %div.46), kind=kOutput, calls=%fused_computation.50 | convolution fusion | flops 1612447744 | bytes 2097160 | tf_op jit(solution)/shard_map/dot_general | solution.py:18
  73.4 1.8 %fusion.92 = f32[512,512]{1,0:T(8,128)S(1)} fusion(f32[512,512]{1,0:T(8,128)S(1)} %fusion.26), kind=kOutput, calls=%fused_computation.129 | convolution fusion | flops 1610612736 | bytes 2097152 | tf_op jit(solution)/shard_map/dot_general | solution.py:18
  75.3 1.9 %fusion.20 = f32[512,512]{1,0:T(8,128)S(1)} fusion(f32[512,512]{1,0:T(8,128)S(1)} %fusion.92, f32[]{:T(128)S(6)} %div.47, f32[512,512]{1,0:T(8,128)S(1)} %get-tuple-element.18, f32[]{:T(128)S(6)} %div.46), kind=kOutput, calls=%fused_computation.44 | convolution fusion | flops 1611661312 | bytes 3145736 | tf_op jit(solution)/shard_map/dot_general | solution.py:18
  77.2 3.0 %fusion.23 = f32[512,512]{1,0:T(8,128)} fusion(f32[512,512]{1,0:T(8,128)S(1)} %fusion.20, f32[]{:T(128)S(6)} %div.47, f32[512,512]{1,0:T(8,128)S(1)} %get-tuple-element.18, f32[]{:T(128)S(6)} %div.46), kind=kOutput, calls=%fused_computation.47 | convolution fusion | flops 1613496320 | bytes 3145736 | tf_op jit(solution)/shard_map/dot_general | solution.py:18
  80.1 1.9 %fusion.22 = f32[512,512]{1,0:T(8,128)S(1)} fusion(f32[512,512]{1,0:T(8,128)S(1)} %fusion.20), kind=kOutput, calls=%fused_computation.46 | convolution fusion | flops 1611661312 | bytes 2097152 | tf_op jit(solution)/shard_map/dot_general | solution.py:18
  82.9 2.0 %fusion.27 = f32[512,512]{1,0:T(8,128)S(1)} fusion(f32[]{:T(128)S(6)} %div.50, f32[512,512]{1,0:T(8,128)S(1)} %get-tuple-element.10, f32[]{:T(128)S(6)} %div.49), kind=kOutput, calls=%fused_computation.51 | convolution fusion | flops 1612447744 | bytes 2097160 | tf_op jit(solution)/shard_map/dot_general | solution.py:18
  84.9 2.1 %fusion.94 = f32[512,512]{1,0:T(8,128)S(1)} fusion(f32[512,512]{1,0:T(8,128)S(1)} %fusion.27), kind=kOutput, calls=%fused_computation.131 | convolution fusion | flops 1610612736 | bytes 2097152 | tf_op jit(solution)/shard_map/dot_general | solution.py:18
  87.0 1.9 %fusion.18 = f32[512,512]{1,0:T(8,128)S(1)} fusion(f32[512,512]{1,0:T(8,128)S(1)} %fusion.94, f32[]{:T(128)S(6)} %div.50, f32[512,512]{1,0:T(8,128)S(1)} %copy-done.2, f32[]{:T(128)S(6)} %div.49), kind=kOutput, calls=%fused_computation.42 | convolution fusion | flops 1611661312 | bytes 3145736 | tf_op jit(solution)/shard_map/dot_general | solution.py:18
  88.9 3.0 %fusion.25 = f32[512,512]{1,0:T(8,128)} fusion(f32[512,512]{1,0:T(8,128)S(1)} %fusion.18, f32[]{:T(128)S(6)} %div.50, f32[512,512]{1,0:T(8,128)S(1)} %copy-done.2, f32[]{:T(128)S(6)} %div.49), kind=kOutput, calls=%fused_computation.49 | convolution fusion | flops 1613496320 | bytes 3145736 | tf_op jit(solution)/shard_map/dot_general | solution.py:18
  91.9 2.9 %fusion.24 = f32[512,512]{1,0:T(8,128)} fusion(f32[512,512]{1,0:T(8,128)S(1)} %fusion.18), kind=kOutput, calls=%fused_computation.48 | convolution fusion | flops 1611661312 | bytes 2097152 | tf_op jit(solution)/shard_map/dot_general | solution.py:18
  94.9 1.8 %fusion.93 = f32[512,512]{1,0:T(8,128)S(1)} fusion(f32[512,512]{1,0:T(8,128)S(1)} %fusion.22), kind=kOutput, calls=%fused_computation.130 | convolution fusion | flops 1610612736 | bytes 2097152 | tf_op jit(solution)/shard_map/dot_general | solution.py:18
  96.7 2.9 %select_subtract_fusion.3 = f32[512,512]{1,0:T(8,128)} fusion(f32[512,512]{1,0:T(8,128)S(1)} %fusion.93, f32[512,512]{1,0:T(8,128)S(1)} %fusion.20), kind=kOutput, calls=%fused_computation.3 | convolution fusion | flops 1611661312 | bytes 3145728 | tf_op jit(solution)/shard_map/dot_general | solution.py:18
  99.7 1.8 %fusion.95 = f32[512,512]{1,0:T(8,128)S(1)} fusion(f32[512,512]{1,0:T(8,128)S(1)} %copy-done), kind=kOutput, calls=%fused_computation.132 | convolution fusion | flops 1610612736 | bytes 2097152 | tf_op jit(solution)/shard_map/dot_general | solution.py:18
  101.5 2.1 %select_subtract_fusion = f32[512,512]{1,0:T(8,128)S(1)} fusion(f32[512,512]{1,0:T(8,128)S(1)} %fusion.95, f32[512,512]{1,0:T(8,128)S(1)} %fusion.18), kind=kOutput, calls=%fused_computation | convolution fusion | flops 1611661312 | bytes 3145728 | tf_op jit(solution)/shard_map/dot_general | solution.py:18
  103.7 3.1 %fusion.1 = bf16[512,512]{1,0:T(8,128)(2,1)S(1)} fusion(f32[512,512]{1,0:T(8,128)} %fusion.23, f32[512,512]{1,0:T(8,128)S(1)} %copy-done.3, f32[]{:T(128)S(6)} %sqrt.24), kind=kOutput, calls=%fused_computation.16 | convolution fusion | flops 1611137024 | bytes 2621444 | tf_op jit(solution)/shard_map/dot_general | solution.py:18
  106.9 5.0 %fusion.31 = (bf16[1,512,512]{2,1,0:T(8,128)(2,1)}, bf16[1,512,512]{2,1,0:T(8,128)(2,1)}, bf16[1,512,512]{2,1,0:T(8,128)(2,1)}, bf16[1,512,512]{2,1,0:T(8,128)(2,1)}) fusion(bf16[512,512]{1,0:T(8,128)(2,1)S(1)} %fusion.1, bf16[2,2,512,512]{3,2,1,0:T(8,128)(2,1)} %param.6, pred[]{:T(512)S(6)} %eq.96, pred[]{:T(512)S(6)} %eq.95, pred[]{:T(512)S(6)} %eq.98, ...), kind=kOutput, calls=%fused_computation.57 | convolution fusion | flops 1613234176 | bytes 6815756 | tf_op jit(solution)/shard_map/dot_general | solution.py:18
  111.9 3.0 %multiply_reduce_fusion = (f32[2]{0:T(128)S(1)}, f32[2,512,512]{2,1,0:T(8,128)S(1)}) fusion(bf16[1,512,512]{2,1,0:T(8,128)(2,1)} %get-tuple-element.14, bf16[1,512,512]{2,1,0:T(8,128)(2,1)} %get-tuple-element.13, bf16[1,512,512]{2,1,0:T(8,128)(2,1)} %get-tuple-element.15, bf16[1,512,512]{2,1,0:T(8,128)(2,1)} %get-tuple-element.16, ...), kind=kOutput, calls=%fused_computation.7 | convolution fusion | flops 1076363264 | bytes 5242888 | tf_op jit(solution)/shard_map/bik,bkj->bij/dot_general | solution.py:81
  115.1 28.8 %all_to_all.22 = f32[8,1,128]{2,1,0:T(1,128)S(1)} all-to-all(f32[8,1,128]{2,1,0:T(1,128)S(1)} %broadcast_in_dim.105), channel_id=1, replica_groups=mesh['z'=4,'y'=4,'x'=4,'h'=4,'c'=2] {'h','c'}, dimensions={0} | all-to-all | bytes 8192 | tf_op jit(solution)/shard_map/all_to_all | solution.py:36
  144.2 1.3 fusion.3
  (53 shorter events, 10.5 us)
Async XLA Ops:
  32.1 20.7 %copy-start.6 = (f32[4]{0:T(128)S(1)}, f32[4]{0:T(128)}, u32[]{:S(2)}) copy-start(f32[4]{0:T(128)} %param.7) | copy-start | bytes 52
  32.1 20.7 %copy-start.7 = (s32[2]{0:T(128)S(1)}, s32[2]{0:T(128)}, u32[]{:S(2)}) copy-start(s32[2]{0:T(128)} %param.8) | copy-start | bytes 28
  32.1 21.5 %copy-start.4 = (bf16[1,2,512,512]{3,2,1,0:T(8,128)(2,1)S(1)}, bf16[1,2,512,512]{3,2,1,0:T(8,128)(2,1)}, u32[]{:S(2)}) copy-start(bf16[1,2,512,512]{3,2,1,0:T(8,128)(2,1)} %param.5) | copy-start | bytes 3145732
  46.2 17.3 %all-to-all-start.2 = ((f32[16,128,128]{2,1,0:T(8,128)}), f32[16,128,128]{2,1,0:T(8,128)S(1)}, u32[]{:S(2)}, u32[]{:S(2)}) async-start(f32[16,128,128]{2,1,0:T(8,128)} %broadcast_in_dim.96), calls=%async_computation.2 | async-start | bytes 2097152 | tf_op jit(solution)/shard_map/all_to_all | solution.py:36
  67.2 15.7 %copy-start.1 = (f32[512,512]{1,0:T(8,128)}, f32[512,512]{1,0:T(8,128)S(1)}, u32[]{:S(2)}) copy-start(f32[512,512]{1,0:T(8,128)S(1)} %get-tuple-element.10) | copy-start | bytes 3145732
  84.9 2.1 %copy-start.2 = (f32[512,512]{1,0:T(8,128)S(1)}, f32[512,512]{1,0:T(8,128)}, u32[]{:S(2)}) copy-start(f32[512,512]{1,0:T(8,128)} %copy-done.1) | copy-start | bytes 3145732
  96.7 2.9 %copy-start = (f32[512,512]{1,0:T(8,128)S(1)}, f32[512,512]{1,0:T(8,128)}, u32[]{:S(2)}) copy-start(f32[512,512]{1,0:T(8,128)} %fusion.24) | copy-start | bytes 3145732
  101.5 2.2 %copy-start.3 = (f32[512,512]{1,0:T(8,128)S(1)}, f32[512,512]{1,0:T(8,128)}, u32[]{:S(2)}) copy-start(f32[512,512]{1,0:T(8,128)} %select_subtract_fusion.3) | copy-start | bytes 3145732
  103.7 3.2 %copy-start.8 = (f32[512,512]{1,0:T(8,128)S(1)}, f32[512,512]{1,0:T(8,128)}, u32[]{:S(2)}) copy-start(f32[512,512]{1,0:T(8,128)} %fusion.25) | copy-start | bytes 3145732
  106.9 5.0 %copy-start.5 = (bf16[1,2,512,512]{3,2,1,0:T(8,128)(2,1)S(1)}, bf16[1,2,512,512]{3,2,1,0:T(8,128)(2,1)}, u32[]{:S(2)}) copy-start(bf16[1,2,512,512]{3,2,1,0:T(8,128)(2,1)} %param.5) | copy-start | bytes 3145732

commit v2 on v1

v2 whole, which is shorter than its diff:
```python
import jax
import jax.numpy as jnp
from jax import lax
from jax.experimental import pallas as pl
from jax.experimental.pallas import tpu as pltpu
from jax.sharding import Mesh, PartitionSpec as P

B = 512
NB = 2
LAYERS = 4
SHARDS = 64
NORM_EPSILON = 1e-06
PLANE = ("y", "x")
COLUMN = ("h", "c")
T = 128
NT = B // T
CHUNKS = 16
ROWS = B // CHUNKS
f32, bf16 = jnp.float32, jnp.bfloat16
VMEM = pl.BlockSpec(memory_space=pltpu.VMEM)
SMEM = pl.BlockSpec(memory_space=pltpu.SMEM)


def params(mib):
    return pltpu.CompilerParams(vmem_limit_bytes=mib << 20)


def dot(a, b):
    return jnp.dot(a, b, preferred_element_type=f32)


def refreshed(owners):
    f = [owners[0, 0] >= 0, owners[0, 1] >= 0, owners[1, 0] >= 0, owners[1, 1] >= 0]
    first = jnp.where(f[0], 0, jnp.where(f[1], 1, 2))
    last = jnp.where(f[3], 3, jnp.where(f[2], 2, 1))
    return first, last


def gram_kernel(owners, g, out, grams, flip):
    for slot, stat in enumerate(refreshed(owners)):
        block = g[stat // 2]

        @pl.when(stat % 2 == 0)
        def _():
            grams[slot] = lax.dot_general(block, block, (((1,), (1,)), ((), ())), preferred_element_type=f32)

        @pl.when(stat % 2 == 1)
        def _():
            flip[...] = block.T
            grams[slot] = dot(flip[...], block)

    row = lax.broadcasted_iota(jnp.int32, (ROWS, B), 0)
    col = lax.broadcasted_iota(jnp.int32, (ROWS, B), 1)
    diag = jnp.zeros((1, B), f32)
    for k in range(CHUNKS):
        rows = slice(k * ROWS, (k + 1) * ROWS)
        a, b = grams[0, rows, :], grams[1, rows, :]
        c = jnp.where(row + k * ROWS >= col, a, b)
        diag = diag + jnp.sum(jnp.where(row + k * ROWS == col, b, 0.0), axis=0, keepdims=True)
        for j in range(NT):
            out[k, j * ROWS : (j + 1) * ROWS, :] = c[:, j * T : (j + 1) * T]
    tail = jnp.concatenate([diag[:, j * T : (j + 1) * T] for j in range(NT)] + [jnp.zeros((4, T), f32)], axis=0)
    for k in range(CHUNKS):
        out[k, T : T + 8, :] = tail


def sum_kernel(parts, out):
    total = parts[0]
    for k in range(1, parts.shape[0]):
        total = total + parts[k]
    for k in range(out.shape[0]):
        out[k] = total


def plane_sum_kernel(parts, out, diag):
    total = parts[0]
    for k in range(1, parts.shape[0]):
        total = total + parts[k]
    diag[...] = total[T:]
    for k in range(out.shape[0]):
        out[k] = total[:T]


def eye_mask():
    return lax.broadcasted_iota(jnp.int32, (T, T), 0) == lax.broadcasted_iota(jnp.int32, (T, T), 1)


def tile(i, j):
    return slice(i * T, (i + 1) * T), slice(j * T, (j + 1) * T)


class Diag:
    def __init__(self, cols, rows):
        self.cols, self.rows = cols, rows

    def map(self, f):
        return Diag([f(c) for c in self.cols], [f(r) for r in self.rows])


def diag_of(blocks, mask):
    picked = [jnp.where(mask, b, 0.0) for b in blocks]
    return Diag(
        [jnp.sum(p, axis=1, keepdims=True) for p in picked],
        [jnp.sum(p, axis=0, keepdims=True) for p in picked],
    )


def split(x):
    hi = x.astype(bf16)
    return hi, (x - hi.astype(f32)).astype(bf16)


def store_right(cat, i, j, x):
    hi, lo = split(x)
    r, c = tile(i, j)
    cat[r, c] = hi
    cat[slice(r.start + B, r.stop + B), c] = lo
    cat[slice(r.start + 2 * B, r.stop + 2 * B), c] = hi


def store_left(cat, i, j, x):
    hi, lo = split(x)
    r, c = tile(i, j)
    cat[r, c] = hi
    cat[r, slice(c.start + B, c.stop + B)] = hi
    cat[r, slice(c.start + 2 * B, c.stop + 2 * B)] = lo


def finish(acc, off, diag_terms, keep, mask):
    blocks = []
    for i in range(NT):
        for j in range(NT):
            r, c = tile(i, j)
            base = acc[r, c]
            full = base + off(i, j)
            if i == j:
                full = jnp.where(mask, base + diag_terms(i), full)
                blocks.append(full)
                keep(i, j, full, jnp.where(mask, 0.0, full))
            else:
                keep(i, j, full, full)
    return diag_of(blocks, mask)


def main_kernel(owners, layers, damping, packed, diag_b, g, prev, update, sums, c_ref, m_ref, mcat, s_ref, shi, f_ref, fcat, h_ref, hcat, roots, accs):
    mask = eye_mask()
    ids = refreshed(owners)
    for k in range(CHUNKS):
        for j in range(NT):
            c_ref[k * ROWS : (k + 1) * ROWS, j * T : (j + 1) * T] = packed[k, j * ROWS : (j + 1) * ROWS, :]
    for n in range(4):
        @pl.when((ids[0] != n) & (ids[1] != n))
        def _():
            roots[n] = prev[n]
    lower = lax.broadcasted_iota(jnp.int32, (T, T), 0) >= lax.broadcasted_iota(jnp.int32, (T, T), 1)
    blocks = [{}, {}]
    diags, scales, shifts, zs = [], [], [], []
    for s in range(2):
        square = jnp.zeros((1, T), f32)
        on_diag = []
        for i in range(NT):
            for j in range(NT):
                r, c = tile(i, j)
                own = (i > j) if s == 0 else (i < j)
                if i == j:
                    b = c_ref[r, c]
                    if s == 0:
                        b = jnp.where(lower, b, b.T)
                    else:
                        b = jnp.where(mask, diag_b[i : i + 1, :], jnp.where(lower, b.T, b))
                    on_diag.append(b)
                elif own:
                    b = c_ref[r, c]
                else:
                    b = c_ref[c, r].T
                b = b * (1.0 / (SHARDS * B))
                m_ref[s, 0, r, c] = b
                square = square + jnp.sum(b * b, axis=0, keepdims=True)
        d = diag_of(on_diag, mask).map(lambda v: v * (1.0 / (SHARDS * B)))
        trace = jnp.sum(d.rows[0] + d.rows[1] + d.rows[2] + d.rows[3], axis=1, keepdims=True)
        layer = layers[ids[s] // 2]
        shift = damping[layer] * trace * (1.0 / B)
        norm = jnp.sum(square, axis=1, keepdims=True) + 2.0 * shift * trace + B * shift * shift
        z = 2.5 / jnp.sqrt(norm)
        d = d.map(lambda v: z * (v + shift))
        for i in range(NT):
            for j in range(NT):
                r, c = tile(i, j)
                b = z * m_ref[s, 0, r, c]
                m_ref[s, 0, r, c] = b
                store_right(mcat.at[s, 0], i, j, jnp.where(mask, 0.0, b) if i == j else b)
        diags.append(d)
        zs.append(z)

    def step(v):
        return 1.25 - 0.25 * v

    dm = list(diags)
    dx = [d.map(step) for d in dm]
    dh = [None, None]
    for it in range(2):
        ds, df = [None, None], [None, None]
        for s in range(2):
            left = mcat[s, it, :B, :]
            accs[s] = dot(left, left) * (1.0 / 16.0)
        for s in range(2):
            d = dx[s]

            def keep(i, j, full, bare, s=s):
                r, c = tile(i, j)
                s_ref[s, r, c] = full
                shi[s, r, c] = bare.astype(bf16)

            ds[s] = finish(
                accs.at[s],
                lambda i, j, s=s, d=d: (-0.25 * m_ref[s, it, tile(i, j)[0], tile(i, j)[1]]) * (d.cols[i] + d.rows[j]),
                lambda i, d=d: d.cols[i] * d.rows[i],
                keep,
                mask,
            )
        for s in range(2):
            accs[s] = dot(shi[s], shi[s])
        for s in range(2):
            d = ds[s]

            def keep(i, j, full, bare, s=s):
                r, c = tile(i, j)
                f_ref[s, r, c] = full
                store_left(fcat.at[s], i, j, bare)

            df[s] = finish(
                accs.at[s],
                lambda i, j, s=s, d=d: s_ref[s, tile(i, j)[0], tile(i, j)[1]] * (d.cols[i] + d.rows[j]),
                lambda i, d=d: d.cols[i] * d.rows[i],
                keep,
                mask,
            )
        for s in range(2):
            accs[s] = dot(fcat[s], mcat[s, it])
        for s in range(2):
            da, db = df[s], dm[s]

            def keep(i, j, full, bare, s=s):
                r, c = tile(i, j)
                m_ref[s, it + 1, r, c] = full
                store_right(mcat.at[s, it + 1], i, j, bare)

            dm[s] = finish(
                accs.at[s],
                lambda i, j, s=s, da=da, db=db: da.cols[i] * m_ref[s, it, tile(i, j)[0], tile(i, j)[1]]
                + f_ref[s, tile(i, j)[0], tile(i, j)[1]] * db.rows[j],
                lambda i, da=da, db=db: da.cols[i] * db.rows[i],
                keep,
                mask,
            )
        old = dx
        dx = [d.map(step) for d in dm]
        if it == 0:
            for s in range(2):
                accs[s] = dot(mcat[s, 0, :B, :], mcat[s, 1, :B, :]) * (1.0 / 16.0)
            for s in range(2):
                da, db = old[s], dx[s]

                def keep(i, j, full, bare, s=s):
                    r, c = tile(i, j)
                    h_ref[s, r, c] = full
                    store_left(hcat.at[s], i, j, bare)

                dh[s] = finish(
                    accs.at[s],
                    lambda i, j, s=s, da=da, db=db: -0.25
                    * (da.cols[i] * m_ref[s, 1, tile(i, j)[0], tile(i, j)[1]] + m_ref[s, 0, tile(i, j)[0], tile(i, j)[1]] * db.rows[j]),
                    lambda i, da=da, db=db: da.cols[i] * db.rows[i],
                    keep,
                    mask,
                )
    for s in range(2):
        accs[s] = dot(hcat[s], mcat[s, 2]) * -0.25
    for s in range(2):
        da, db = dh[s], dx[s]
        scale = jnp.sqrt(jnp.sqrt(zs[s]))

        def keep(i, j, full, bare, s=s, scale=scale):
            r, c = tile(i, j)
            roots[ids[s], r, c] = (scale * full).astype(bf16)

        finish(
            accs.at[s],
            lambda i, j, s=s, da=da, db=db: da.cols[i] * (-0.25 * m_ref[s, 2, tile(i, j)[0], tile(i, j)[1]])
            + h_ref[s, tile(i, j)[0], tile(i, j)[1]] * db.rows[j],
            lambda i, da=da, db=db: da.cols[i] * db.rows[i],
            keep,
            mask,
        )
    lane = lax.broadcasted_iota(jnp.int32, (8, T), 1)
    line = lax.broadcasted_iota(jnp.int32, (8, T), 0)
    tail = jnp.zeros((8, T), f32)
    for b in range(NB):
        half = dot(roots[2 * b], g[b]).astype(bf16)
        u = dot(half, roots[2 * b + 1])
        update[b] = u
        x = g[b].astype(f32)
        gs = jnp.sum(jnp.sum(x * x, axis=0, keepdims=True), axis=1, keepdims=True)
        us = jnp.sum(jnp.sum(u * u, axis=0, keepdims=True), axis=1, keepdims=True)
        hit = lane == layers[b]
        tail = tail + jnp.where(hit & (line == 0), gs, 0.0) + jnp.where(hit & (line == 1), us, 0.0)
    for k in range(sums.shape[0]):
        sums[k] = tail


def scale_kernel(layers, sums, update, out):
    total = sums[0]
    for k in range(1, sums.shape[0]):
        total = total + sums[k]
    ratio = jnp.sqrt((total[0:1] + NORM_EPSILON) / (total[1:2] + NORM_EPSILON))
    lane = lax.broadcasted_iota(jnp.int32, (1, T), 1)
    for b in range(NB):
        mine = jnp.sum(jnp.where(lane == layers[b], ratio, 0.0), axis=1, keepdims=True)
        out[0, b] = (update[b] * mine).astype(bf16)


def per_device(grads, prev_roots, damping, block_layer, owners):
    g = grads[0]
    prev = prev_roots.reshape(2 * NB, B, B)
    shape = jax.ShapeDtypeStruct
    packed = pl.pallas_call(
        gram_kernel,
        out_shape=shape((CHUNKS, T + 8, T), f32),
        in_specs=[SMEM, VMEM],
        out_specs=VMEM,
        scratch_shapes=[pltpu.VMEM((2, B, B), f32), pltpu.VMEM((B, B), bf16)],
        compiler_params=params(16),
        name="gram",
    )(owners, g)
    packed = lax.all_to_all(packed, PLANE, 0, 0)
    packed = pl.pallas_call(
        sum_kernel, out_shape=shape((4, T + 8, T), f32), in_specs=[VMEM], out_specs=VMEM, compiler_params=params(16), name="plane_sum"
    )(packed)
    packed = lax.all_to_all(packed, "z", 0, 0)
    packed, diag_b = pl.pallas_call(
        plane_sum_kernel,
        out_shape=[shape((CHUNKS, T, T), f32), shape((8, T), f32)],
        in_specs=[VMEM],
        out_specs=[VMEM, VMEM],
        compiler_params=params(16),
        name="line_sum",
    )(packed)
    packed = lax.all_to_all(packed, PLANE, 0, 0)
    update, sums = pl.pallas_call(
        main_kernel,
        out_shape=[shape((NB, B, B), f32), shape((8, 8, T), f32)],
        in_specs=[SMEM, SMEM, SMEM, VMEM, VMEM, VMEM, VMEM],
        out_specs=[VMEM, VMEM],
        scratch_shapes=[
            pltpu.VMEM((B, B), f32),
            pltpu.VMEM((2, 3, B, B), f32),
            pltpu.VMEM((2, 3, 3 * B, B), bf16),
            pltpu.VMEM((2, B, B), f32),
            pltpu.VMEM((2, B, B), bf16),
            pltpu.VMEM((2, B, B), f32),
            pltpu.VMEM((2, B, 3 * B), bf16),
            pltpu.VMEM((2, B, B), f32),
            pltpu.VMEM((2, B, 3 * B), bf16),
            pltpu.VMEM((4, B, B), bf16),
            pltpu.VMEM((2, B, B), f32),
        ],
        compiler_params=params(48),
        name="roots_and_update",
    )(owners, block_layer, damping, packed, diag_b, g, prev)
    sums = lax.all_to_all(sums, COLUMN, 0, 0)
    return pl.pallas_call(
        scale_kernel,
        out_shape=shape((1, NB, B, B), bf16),
        in_specs=[SMEM, VMEM, VMEM],
        out_specs=VMEM,
        compiler_params=params(16),
        name="graft",
    )(block_layer, sums, update)


def solution(mesh):
    dp, mp = ("z", "y", "x"), ("h", "c")
    fine = Mesh(mesh.devices.reshape(4, 4, 4, 4, 2), dp + mp)
    return jax.shard_map(
        per_device,
        mesh=fine,
        in_specs=(P(dp, mp, None, None), P(mp, None, None, None), P(), P(mp), P(mp, None)),
        out_specs=P(dp, mp, None, None),
        check_vma=False,
    )
```

time: 146 us -> 102 us (0.70)
  matrix products: 43.3 us -> 0 us
  Pallas kernels: 0 us -> 17.9 us
  blocking collectives: 65.3 us -> 81.7 us
  between operations: 10.7 us -> 0.04 us
  waiting for transfers between devices: 9.38 us -> 0 us
  other arithmetic: 7.7 us -> 0 us
  starting transfers between devices: 3.84 us -> 0 us
  local copies, waits for them, and re-layouts: 5.35 us -> 1.92 us
    dot_general x19 -> x0, matrix products: 43.3 us -> none  [the longest x16 39.3 us: mm(): return jnp.dot(a, b, precision=HIGHEST, preferred_element_type=jnp.float32)]
    pallas_call x0 -> x5, Pallas kernels: none -> 17.9 us  [the longest x1 14.3 us: per_device(): pl.pallas_call(main_kernel, out_shape=[shape((NB, B, B), f32), shape((8,...]
    all_to_all x3 -> x4, blocking collectives: 65.3 us -> 81.7 us  [the longest x2 39.8 us: per_device(): packed = lax.all_to_all(packed, PLANE, 0, 0)]
    all_to_all x1 -> x0, waiting for transfers between devices: 9.38 us -> none  [spread(): lax.all_to_all(jnp.broadcast_to(a[None], (count,) + a.shape), axes, 0, 0)]
    reduce_sum x9 -> x0, other arithmetic: 4.08 us -> none  [the longest x1 2.19 us: root(): damp = block_damp[stat // 2] * jnp.trace(statistic) / B]
    all_to_all x1 -> x0, starting transfers between devices: 3.84 us -> none  [spread(): lax.all_to_all(jnp.broadcast_to(a[None], (count,) + a.shape), axes, 0, 0)]
    unnamed x18 -> x12, local copies, waits for them, and re-layouts: 0.05 us -> 1.92 us
    squeeze x3 -> x0, local copies, waits for them, and re-layouts: 1.7 us -> none  [gram(): block = g[stat // 2]]
  transfers between devices with their start and end apart: 1 -> 0, of which waited for: 1 -> 0; matrix products, arithmetic and copies ran while one was open for 1% -> 0% of each run, Pallas kernels for 0% -> 0%
where the time goes in v2:
time: 102 us
  blocking collectives  81.7 us (80%)
  Pallas kernels  17.9 us (18%)
  local copies, waits for them, and re-layouts  1.92 us (2%)
    all_to_all x2, blocking collectives, per_device(): packed = lax.all_to_all(packed, PLANE, 0, 0)  39.8 us
    all_to_all x1, blocking collectives, per_device(): sums = lax.all_to_all(sums, COLUMN, 0, 0)  29 us
    pallas_call x1, Pallas kernels, per_device(): pl.pallas_call(main_kernel, out_shape=[shape((NB, B, B), f32), shape((8,...  14.3 us
    all_to_all x1, blocking collectives, per_device(): packed = lax.all_to_all(packed, 'z', 0, 0)  12.9 us

profile of v2, /device:TPU:1, one launch (start us, length us, event | category | flops | bytes accessed | tf_op | source)
XLA Modules:
  0.0 101.6 jit_solution(15048569179882373405)
XLA Ops:
  0.0 0.0 copy-start
  0.0 1.2 %copy-done = bf16[1,2,512,512]{3,2,1,0:T(8,128)(2,1)S(1)} copy-done((bf16[1,2,512,512]{3,2,1,0:T(8,128)(2,1)S(1)}, bf16[1,2,512,512]{3,2,1,0:T(8,128)(2,1)}, u32[]{:S(2)}) %copy-start) | copy-done | bytes 1048600
  1.2 0.0 copy-start.2
  1.2 0.7 copy-done.2
  1.9 1.7 %gram.1 = f32[16,136,128]{2,1,0:T(8,128)S(1)} custom-call(s32[2,2]{1,0:T(2,128)S(1)} %copy-done.2, bf16[2,512,512]{2,1,0:T(8,128)(2,1)S(1)} %bitcast.2), custom_call_target="tpu_custom_call" | custom-call | tf_op jit(solution)/shard_map/gram/pallas_call | solution.py:326
  3.6 23.5 %all_to_all.20.parts = f32[16,136,128]{2,1,0:T(8,128)S(1)} all-to-all(f32[16,136,128]{2,1,0:T(8,128)S(1)} %gram.1), channel_id=1, replica_groups=mesh['z'=4,'y'=4,'x'=4,'h'=4,'c'=2] {'y','x'}, dimensions={0} | all-to-all | bytes 2228224 | tf_op jit(solution)/shard_map/all_to_all | solution.py:335
  27.1 0.0 copy-start.1
  27.1 0.0 copy-start.3
  27.1 0.0 copy-start.4
  27.1 0.0 copy-start.5
  27.1 0.1 plane_sum.1
  27.2 12.9 %all_to_all.21.parts = f32[4,136,128]{2,1,0:T(8,128)S(1)} all-to-all(f32[4,136,128]{2,1,0:T(8,128)S(1)} %plane_sum.1), channel_id=1, replica_groups=mesh['z'=4,'y'=4,'x'=4,'h'=4,'c'=2] {'z'}, dimensions={0} | all-to-all | bytes 557056 | tf_op jit(solution)/shard_map/all_to_all | solution.py:339
  40.1 0.1 line_sum.1
  40.2 16.3 %all_to_all.22.packed = f32[16,128,128]{2,1,0:T(8,128)S(1)} all-to-all(f32[16,128,128]{2,1,0:T(8,128)S(1)} %get-tuple-element.9), channel_id=1, replica_groups=mesh['z'=4,'y'=4,'x'=4,'h'=4,'c'=2] {'y','x'}, dimensions={0} | all-to-all | bytes 2097152 | tf_op jit(solution)/shard_map/all_to_all | solution.py:348
  56.5 0.0 copy-done.1
  56.5 0.0 copy-done.3
  56.5 0.0 copy-done.4
  56.5 0.0 copy-done.5
  56.5 14.3 %roots_and_update.1 = (f32[2,512,512]{2,1,0:T(8,128)S(1)}, f32[8,8,128]{2,1,0:T(8,128)S(1)}) custom-call(s32[2,2]{1,0:T(2,128)S(1)} %copy-done.3, s32[2]{0:T(128)S(1)} %copy-done.4, f32[4]{0:T(128)S(1)} %copy-done.5, f32[16,128,128]{2,1,0:T(8,128)S(1)} %all_to_all.22.packed, f32[8,128]{1,0:T(8,128)S(1)} %get-tuple-element.10.diag_b, ...), custom_call_target="tpu_custom_call" | custom-call | tf_op jit(solution)/shard_map/roots_and_update/pallas_call | solution.py:349
  70.8 29.0 %all_to_all.23.sums = f32[8,8,128]{2,1,0:T(8,128)S(1)} all-to-all(f32[8,8,128]{2,1,0:T(8,128)S(1)} %get-tuple-element.11), channel_id=1, replica_groups=mesh['z'=4,'y'=4,'x'=4,'h'=4,'c'=2] {'h','c'}, dimensions={0} | all-to-all | bytes 65536 | tf_op jit(solution)/shard_map/all_to_all | solution.py:370
  99.8 1.8 %graft.1 = bf16[1,2,512,512]{3,2,1,0:T(8,128)(2,1)} custom-call(s32[2]{0:T(128)S(1)} %copy-done.4, f32[8,8,128]{2,1,0:T(8,128)S(1)} %all_to_all.23.sums, f32[2,512,512]{2,1,0:T(8,128)S(1)} %get-tuple-element.12.update), custom_call_target="tpu_custom_call" | custom-call | tf_op jit(solution)/shard_map/graft/pallas_call | solution.py:371
Async XLA Ops:
  0.0 1.2 %copy-start = (bf16[1,2,512,512]{3,2,1,0:T(8,128)(2,1)S(1)}, bf16[1,2,512,512]{3,2,1,0:T(8,128)(2,1)}, u32[]{:S(2)}) copy-start(bf16[1,2,512,512]{3,2,1,0:T(8,128)(2,1)} %param.5) | copy-start | bytes 3145732
  1.2 0.7 copy-start.2
  27.1 29.4 %copy-start.1 = (bf16[1,2,512,512]{3,2,1,0:T(8,128)(2,1)S(1)}, bf16[1,2,512,512]{3,2,1,0:T(8,128)(2,1)}, u32[]{:S(2)}) copy-start(bf16[1,2,512,512]{3,2,1,0:T(8,128)(2,1)} %param.5) | copy-start | bytes 3145732
  27.1 29.4 %copy-start.3 = (s32[2,2]{1,0:T(2,128)S(1)}, s32[2,2]{1,0:T(2,128)}, u32[]{:S(2)}) copy-start(s32[2,2]{1,0:T(2,128)} %owners.3) | copy-start | bytes 52
  27.1 29.4 %copy-start.4 = (s32[2]{0:T(128)S(1)}, s32[2]{0:T(128)}, u32[]{:S(2)}) copy-start(s32[2]{0:T(128)} %layers.3) | copy-start | bytes 28
  27.1 29.4 %copy-start.5 = (f32[4]{0:T(128)S(1)}, f32[4]{0:T(128)}, u32[]{:S(2)}) copy-start(f32[4]{0:T(128)} %damping.1) | copy-start | bytes 52

commit v3 on v1

v3 whole, which is shorter than its diff:
```python
import jax
import jax.numpy as jnp
from jax import lax
from jax.experimental import pallas as pl
from jax.experimental.pallas import tpu as pltpu
from jax.sharding import Mesh, PartitionSpec as P

B = 512
NB = 2
LAYERS = 4
SHARDS = 64
NORM_EPSILON = 1e-06
PLANE = ("y", "x")
COLUMN = ("h", "c")
T = 128
NT = B // T
CHUNKS = 16
ROWS = B // CHUNKS
SPAN = 240.0
TINY = 1e-30
f32, bf16 = jnp.float32, jnp.bfloat16
VMEM = pl.BlockSpec(memory_space=pltpu.VMEM)
SMEM = pl.BlockSpec(memory_space=pltpu.SMEM)
ANY = pl.BlockSpec(memory_space=pl.ANY)


def params(mib):
    return pltpu.CompilerParams(vmem_limit_bytes=mib << 20)


def dot(a, b):
    return jnp.dot(a, b, preferred_element_type=f32)


def refreshed(owners):
    f = [owners[0, 0] >= 0, owners[0, 1] >= 0, owners[1, 0] >= 0, owners[1, 1] >= 0]
    first = jnp.where(f[0], 0, jnp.where(f[1], 1, 2))
    last = jnp.where(f[3], 3, jnp.where(f[2], 2, 1))
    return first, last


def top_of(x):
    top = jnp.max(jnp.max(jnp.abs(x), axis=0, keepdims=True), axis=1, keepdims=True)
    return jnp.maximum(top * 1.008, TINY).astype(bf16).astype(f32)


def encode(x, gain):
    size = jnp.exp2(jnp.minimum(jnp.abs(x) * gain, SPAN) - SPAN / 2)
    return jnp.where(x < 0, -size, size).astype(bf16)


def decode(code, top):
    code = code.astype(f32)
    size = (jnp.log2(jnp.abs(code)) + SPAN / 2) * top
    return jnp.where(code < 0, -size, size)


def parts3(x):
    hi = x.astype(bf16).astype(f32)
    mid = (x - hi).astype(bf16).astype(f32)
    return [hi, mid, x - hi - mid]


def tail_of(diag, top):
    return jnp.concatenate(parts3(diag) + [jnp.broadcast_to(top, (4, T))], axis=0).astype(bf16)


def read_tail(tail):
    tail = tail.astype(f32)
    return tail[0:4] + tail[4:8] + tail[8:12], tail[12:13] * (1.0 / SPAN)


def gram_kernel(owners, g_hbm, out, g, grams, flip, sems):
    copies = [pltpu.make_async_copy(g_hbm.at[0, b], g.at[b], sems.at[b]) for b in range(NB)]
    for c in copies:
        c.start()
    for c in copies:
        c.wait()
    for slot, stat in enumerate(refreshed(owners)):
        block = g[stat // 2]

        @pl.when(stat % 2 == 0)
        def _():
            grams[slot] = lax.dot_general(block, block, (((1,), (1,)), ((), ())), preferred_element_type=f32)

        @pl.when(stat % 2 == 1)
        def _():
            flip[...] = block.T
            grams[slot] = dot(flip[...], block)

    row = lax.broadcasted_iota(jnp.int32, (ROWS, B), 0)
    col = lax.broadcasted_iota(jnp.int32, (ROWS, B), 1)
    diag = [jnp.zeros((1, B), f32), jnp.zeros((1, B), f32)]
    most = [jnp.zeros((ROWS, B), f32), jnp.zeros((ROWS, B), f32)]
    for k in range(CHUNKS):
        rows = slice(k * ROWS, (k + 1) * ROWS)
        a, b = grams[0, rows, :], grams[1, rows, :]
        on = row + k * ROWS == col
        lower = row + k * ROWS > col
        upper = row + k * ROWS < col
        diag[0] = diag[0] + jnp.sum(jnp.where(on, a, 0.0), axis=0, keepdims=True)
        diag[1] = diag[1] + jnp.sum(jnp.where(on, b, 0.0), axis=0, keepdims=True)
        most[0] = jnp.maximum(most[0], jnp.where(lower, jnp.abs(a), 0.0))
        most[1] = jnp.maximum(most[1], jnp.where(upper, jnp.abs(b), 0.0))
    tops = [top_of(m) for m in most]
    gains = [SPAN / t for t in tops]
    for k in range(CHUNKS):
        rows = slice(k * ROWS, (k + 1) * ROWS)
        lower = row + k * ROWS >= col
        c = jnp.where(lower, grams[0, rows, :], grams[1, rows, :])
        c = encode(c, jnp.where(lower, gains[0], gains[1]))
        for j in range(NT):
            out[k, j * ROWS : (j + 1) * ROWS, :] = c[:, j * T : (j + 1) * T]
    tails = []
    for s in range(2):
        d = jnp.concatenate([diag[s][:, j * T : (j + 1) * T] for j in range(NT)], axis=0)
        tails.append(tail_of(d, tops[s]))
    for k in range(CHUNKS):
        out[k, T : T + 16, :] = tails[0]
        out[k, T + 16 : T + 32, :] = tails[1]


def chunk_place():
    mine = lax.axis_index("y") * 4 + lax.axis_index("x")
    r = lax.broadcasted_iota(jnp.int32, (T, T), 0)
    return mine * ROWS + r % ROWS, (r // ROWS) * T + lax.broadcasted_iota(jnp.int32, (T, T), 1)


def add_parts(parts, lower):
    total = jnp.zeros((T, T), f32)
    diag = [jnp.zeros((4, T), f32), jnp.zeros((4, T), f32)]
    for p in range(parts.shape[0]):
        da, ta = read_tail(parts[p, T : T + 16, :])
        db, tb = read_tail(parts[p, T + 16 : T + 32, :])
        total = total + decode(parts[p, :T, :], jnp.where(lower, ta, tb))
        diag = [diag[0] + da, diag[1] + db]
    return total, diag


def code_total(total, row, col):
    tops = [top_of(jnp.where(row > col, total, 0.0)), top_of(jnp.where(row < col, total, 0.0))]
    return encode(total, jnp.where(row >= col, SPAN / tops[0], SPAN / tops[1])), tops


def plane_sum_kernel(parts, out):
    row, col = chunk_place()
    total, diag = add_parts(parts, row >= col)
    code, tops = code_total(total, row, col)
    tails = [tail_of(diag[s], tops[s]) for s in range(2)]
    for k in range(out.shape[0]):
        out[k, :T, :] = code
        out[k, T : T + 16, :] = tails[0]
        out[k, T + 16 : T + 32, :] = tails[1]


def line_sum_kernel(parts, out, diag_out):
    row, col = chunk_place()
    total, diag = add_parts(parts, row >= col)
    code, tops = code_total(total, row, col)
    diag_out[0] = diag[0]
    diag_out[1] = diag[1]
    line = lax.broadcasted_iota(jnp.int32, (16, T), 0)
    tail = jnp.where(line < 8, tops[0], tops[1]).astype(bf16)
    for k in range(out.shape[0]):
        out[k, :T, :] = code
        out[k, T : T + 16, :] = tail


def tile(i, j):
    return slice(i * T, (i + 1) * T), slice(j * T, (j + 1) * T)


class Diag:
    def __init__(self, cols, rows):
        self.cols, self.rows = cols, rows

    def map(self, f):
        return Diag([f(c) for c in self.cols], [f(r) for r in self.rows])


def main_kernel(owners, layers, damping, packed, diags, g, prev, update, sums, c_ref, x_ref, xo, s_ref, so, f_ref, fo, h_ref, ho, roots, accs, sem):
    fetch = pltpu.make_async_copy(prev, roots, sem)
    fetch.start()
    row = lax.broadcasted_iota(jnp.int32, (T, T), 0)
    col = lax.broadcasted_iota(jnp.int32, (T, T), 1)
    mask = row == col
    lower = row > col
    ids = refreshed(owners)
    crow = lax.broadcasted_iota(jnp.int32, (ROWS, T), 0)
    ccol = lax.broadcasted_iota(jnp.int32, (ROWS, T), 1)
    squares = [jnp.zeros((ROWS, T), f32), jnp.zeros((ROWS, T), f32)]
    for k in range(CHUNKS):
        tail = packed[k, T : T + 16, :].astype(f32) * (1.0 / (SPAN * SHARDS * B))
        ta, tb = tail[0:1], tail[8:9]
        for j in range(NT):
            code = packed[k, j * ROWS : (j + 1) * ROWS, :]
            low, high = k * ROWS - j * T - (T - 1), k * ROWS + ROWS - 1 - j * T
            if low > 0:
                x = decode(code, ta)
                squares[0] = squares[0] + x * x
            elif high < 0:
                x = decode(code, tb)
                squares[1] = squares[1] + x * x
            else:
                r, c = crow + k * ROWS, ccol + j * T
                x = decode(code, jnp.where(r > c, ta, tb))
                x = jnp.where(r == c, 0.0, x)
                q = x * x
                squares[0] = squares[0] + jnp.where(r > c, q, 0.0)
                squares[1] = squares[1] + jnp.where(r > c, 0.0, q)
            c_ref[k * ROWS : (k + 1) * ROWS, j * T : (j + 1) * T] = x

    def total(v):
        return jnp.sum(jnp.sum(v, axis=0, keepdims=True), axis=1, keepdims=True)

    def column(r):
        return jnp.sum(jnp.where(mask, r, 0.0), axis=1, keepdims=True)

    dx, scales = [None, None], [None, None]
    for s in range(2):
        d = diags[s] * (1.0 / (SHARDS * B))
        trace = total(d)
        shift = damping[layers[ids[s] // 2]] * trace * (1.0 / B)
        d = d + shift
        z = 2.5 / jnp.sqrt(2.0 * total(squares[s]) + total(d * d))
        scales[s] = jnp.sqrt(jnp.sqrt(z))
        rows = [1.25 - 0.25 * (z * d[i : i + 1, :]) for i in range(NT)]
        dx[s] = Diag([column(r) for r in rows], rows)
        w = -0.25 * z
        for i in range(NT):
            for j in range(i + 1):
                r, c = tile(i, j)
                if i == j:
                    x = c_ref[r, c]
                    x = jnp.where(lower if s == 0 else row < col, x, x.T) * w
                    x_ref[s, 0, r, c] = x
                    xo[s, 0, r, c] = x.astype(bf16)
                else:
                    x = (c_ref[r, c] if s == 0 else c_ref[c, r]) * w
                    a, b = ((r, c), (c, r)) if s == 0 else ((c, r), (r, c))
                    x_ref[s, 0, a[0], a[1]] = x
                    xo[s, 0, a[0], a[1]] = x.astype(bf16)
                    x = x.T
                    x_ref[s, 0, b[0], b[1]] = x
                    xo[s, 0, b[0], b[1]] = x.astype(bf16)

    def finish(acc, off, da, db, keep):
        diag = Diag([], [])
        for i in range(NT):
            for j in range(NT):
                r, c = tile(i, j)
                base = acc[r, c]
                if i == j:
                    on = jnp.where(mask, base, 0.0)
                    diag.cols.append(jnp.sum(on, axis=1, keepdims=True) + da.cols[i] * db.cols[i])
                    diag.rows.append(jnp.sum(on, axis=0, keepdims=True) + da.rows[i] * db.rows[i])
                    keep(r, c, jnp.where(mask, 0.0, base + off(i, j, r, c)), diag.rows[i])
                else:
                    keep(r, c, base + off(i, j, r, c), None)
        return diag

    def square_off(d, ref):
        return lambda i, j, r, c: ref[r, c] * (d.cols[i] + d.rows[j])

    def cross_off(da, aref, db, bref):
        return lambda i, j, r, c: da.cols[i] * bref[r, c] + aref[r, c] * db.rows[j]

    def keep_in(full, off):
        def keep(r, c, x, on):
            full[r, c] = x
            off[r, c] = x.astype(bf16)

        return keep

    first = dx
    for it in range(2):
        ds, df = [None, None], [None, None]
        for s in range(2):
            accs[s] = dot(xo[s, it], xo[s, it])
            ds[s] = finish(accs.at[s], square_off(dx[s], x_ref.at[s, it]), dx[s], dx[s], keep_in(s_ref.at[s], so.at[s]))
        for s in range(2):
            accs[s] = dot(so[s], so[s])
            df[s] = finish(accs.at[s], square_off(ds[s], s_ref.at[s]), ds[s], ds[s], keep_in(f_ref.at[s], fo.at[s]))
        new = [None, None]
        for s in range(2):
            accs[s] = dot(fo[s], xo[s, it])
            dy = dx[s].map(lambda v: v - 1.25)
            new[s] = finish(
                accs.at[s], cross_off(df[s], f_ref.at[s], dy, x_ref.at[s, it]), df[s], dy, keep_in(x_ref.at[s, it + 1], xo.at[s, it + 1])
            ).map(lambda v: v + 1.25)
        dx = new
        if it == 0:
            dh = [None, None]
            for s in range(2):
                accs[s] = dot(xo[s, 0], xo[s, 1])
                dh[s] = finish(
                    accs.at[s], cross_off(first[s], x_ref.at[s, 0], dx[s], x_ref.at[s, 1]), first[s], dx[s], keep_in(h_ref.at[s], ho.at[s])
                )
    fetch.wait()
    for s in range(2):
        accs[s] = dot(ho[s], xo[s, 2])

        def keep(r, c, x, on, s=s):
            if on is not None:
                x = jnp.where(mask, on, x)
            roots[ids[s], r, c] = (x * scales[s]).astype(bf16)

        finish(accs.at[s], cross_off(dh[s], h_ref.at[s], dx[s], x_ref.at[s, 2]), dh[s], dx[s], keep)
    lane = lax.broadcasted_iota(jnp.int32, (8, T), 1)
    line = lax.broadcasted_iota(jnp.int32, (8, T), 0)
    tail = jnp.zeros((8, T), f32)
    for b in range(NB):
        half = dot(roots[2 * b], g[b]).astype(bf16)
        u = dot(half, roots[2 * b + 1])
        update[b] = u
        x = g[b].astype(f32)
        hit = lane == layers[b]
        tail = tail + jnp.where(hit & (line == 0), total(x * x), 0.0) + jnp.where(hit & (line == 1), total(u * u), 0.0)
    for k in range(sums.shape[0]):
        sums[k] = tail


def scale_kernel(layers, sums, update, out, scaled, sems):
    total = sums[0]
    for k in range(1, sums.shape[0]):
        total = total + sums[k]
    ratio = jnp.sqrt((total[0:1] + NORM_EPSILON) / (total[1:2] + NORM_EPSILON))
    lane = lax.broadcasted_iota(jnp.int32, (1, T), 1)
    copies = []
    for b in range(NB):
        mine = jnp.sum(jnp.where(lane == layers[b], ratio, 0.0), axis=1, keepdims=True)
        for h in range(2):
            rows = pl.ds(h * (B // 2), B // 2)
            scaled[b, rows, :] = (update[b, rows, :] * mine).astype(bf16)
            copies.append(pltpu.make_async_copy(scaled.at[b, rows], out.at[0, b, rows], sems.at[2 * b + h]))
            copies[-1].start()
    for c in copies:
        c.wait()


def per_device(grads, prev_roots, damping, block_layer, owners):
    prev = prev_roots.reshape(2 * NB, B, B)
    shape = jax.ShapeDtypeStruct
    packed = pl.pallas_call(
        gram_kernel,
        out_shape=shape((CHUNKS, T + 32, T), bf16),
        in_specs=[SMEM, ANY],
        out_specs=VMEM,
        scratch_shapes=[pltpu.VMEM((NB, B, B), bf16), pltpu.VMEM((2, B, B), f32), pltpu.VMEM((B, B), bf16), pltpu.SemaphoreType.DMA((NB,))],
        compiler_params=params(16),
        name="gram",
    )(owners, grads)
    packed = lax.all_to_all(packed, PLANE, 0, 0)
    packed = pl.pallas_call(
        plane_sum_kernel, out_shape=shape((4, T + 32, T), bf16), in_specs=[VMEM], out_specs=VMEM, compiler_params=params(16), name="plane_sum"
    )(packed)
    packed = lax.all_to_all(packed, "z", 0, 0)
    packed, diags = pl.pallas_call(
        line_sum_kernel,
        out_shape=[shape((CHUNKS, T + 16, T), bf16), shape((2, 4, T), f32)],
        in_specs=[VMEM],
        out_specs=[VMEM, VMEM],
        compiler_params=params(16),
        name="line_sum",
    )(packed)
    packed = lax.all_to_all(packed, PLANE, 0, 0)
    update, sums = pl.pallas_call(
        main_kernel,
        out_shape=[shape((NB, B, B), f32), shape((8, 8, T), f32)],
        in_specs=[SMEM, SMEM, SMEM, VMEM, VMEM, VMEM, ANY],
        out_specs=[VMEM, VMEM],
        scratch_shapes=[
            pltpu.VMEM((B, B), f32),
            pltpu.VMEM((2, 3, B, B), f32),
            pltpu.VMEM((2, 3, B, B), bf16),
            pltpu.VMEM((2, B, B), f32),
            pltpu.VMEM((2, B, B), bf16),
            pltpu.VMEM((2, B, B), f32),
            pltpu.VMEM((2, B, B), bf16),
            pltpu.VMEM((2, B, B), f32),
            pltpu.VMEM((2, B, B), bf16),
            pltpu.VMEM((4, B, B), bf16),
            pltpu.VMEM((2, B, B), f32),
            pltpu.SemaphoreType.DMA,
        ],
        compiler_params=params(40),
        name="roots_and_update",
    )(owners, block_layer, damping, packed, diags, grads[0], prev)
    sums = lax.all_to_all(sums, COLUMN, 0, 0)
    return pl.pallas_call(
        scale_kernel,
        out_shape=shape((1, NB, B, B), bf16),
        in_specs=[SMEM, VMEM, VMEM],
        out_specs=ANY,
        scratch_shapes=[pltpu.VMEM((NB, B, B), bf16), pltpu.SemaphoreType.DMA((2 * NB,))],
        compiler_params=params(16),
        name="graft",
    )(block_layer, sums, update)


def solution(mesh):
    dp, mp = ("z", "y", "x"), ("h", "c")
    fine = Mesh(mesh.devices.reshape(4, 4, 4, 4, 2), dp + mp)
    return jax.shard_map(
        per_device,
        mesh=fine,
        in_specs=(P(dp, mp, None, None), P(mp, None, None, None), P(), P(mp), P(mp, None)),
        out_specs=P(dp, mp, None, None),
        check_vma=False,
    )
```

time: 146 us -> 87.7 us (0.60)
  matrix products: 43.3 us -> 0 us
  Pallas kernels: 0 us -> 13.6 us
  between operations: 10.7 us -> 0.09 us
  waiting for transfers between devices: 9.38 us -> 0 us
  other arithmetic: 7.7 us -> 0 us
  blocking collectives: 65.3 us -> 71.7 us
  starting transfers between devices: 3.84 us -> 0 us
  local copies, waits for them, and re-layouts: 5.35 us -> 1.93 us
    dot_general x19 -> x0, matrix products: 43.3 us -> none  [the longest x16 39.3 us: mm(): return jnp.dot(a, b, precision=HIGHEST, preferred_element_type=jnp.float32)]
    pallas_call x0 -> x5, Pallas kernels: none -> 13.6 us  [the longest x1 8.69 us: per_device(): pl.pallas_call(main_kernel, out_shape=[shape((NB, B, B), f32), shape((8,...]
    all_to_all x1 -> x0, waiting for transfers between devices: 9.38 us -> none  [spread(): lax.all_to_all(jnp.broadcast_to(a[None], (count,) + a.shape), axes, 0, 0)]
    all_to_all x3 -> x4, blocking collectives: 65.3 us -> 71.7 us  [the longest x2 30.9 us: per_device(): packed = lax.all_to_all(packed, PLANE, 0, 0)]
    reduce_sum x9 -> x0, other arithmetic: 4.08 us -> none  [the longest x1 2.19 us: root(): damp = block_damp[stat // 2] * jnp.trace(statistic) / B]
    all_to_all x1 -> x0, starting transfers between devices: 3.84 us -> none  [spread(): lax.all_to_all(jnp.broadcast_to(a[None], (count,) + a.shape), axes, 0, 0)]
    unnamed x18 -> x14, local copies, waits for them, and re-layouts: 0.05 us -> 1.93 us
    squeeze x3 -> x0, local copies, waits for them, and re-layouts: 1.7 us -> none  [gram(): block = g[stat // 2]]
  transfers between devices with their start and end apart: 1 -> 0, of which waited for: 1 -> 0; matrix products, arithmetic and copies ran while one was open for 1% -> 0% of each run, Pallas kernels for 0% -> 0%
where the time goes in v3:
time: 87.7 us; the launch traced here: 87.4 us
  blocking collectives  71.7 us (82%)
  Pallas kernels  13.6 us (16%)
  local copies, waits for them, and re-layouts  1.93 us (2%)
    all_to_all x2, blocking collectives, per_device(): packed = lax.all_to_all(packed, PLANE, 0, 0)  30.9 us
    all_to_all x1, blocking collectives, per_device(): sums = lax.all_to_all(sums, COLUMN, 0, 0)  28.8 us
    all_to_all x1, blocking collectives, per_device(): packed = lax.all_to_all(packed, 'z', 0, 0)  12 us
    pallas_call x1, Pallas kernels, per_device(): pl.pallas_call(main_kernel, out_shape=[shape((NB, B, B), f32), shape((8,...  8.69 us
    pallas_call x1, Pallas kernels, per_device(): pl.pallas_call(gram_kernel, out_shape=shape((CHUNKS, T + 32, T), bf16), i...  2.38 us
    unnamed x14, local copies, waits for them, and re-layouts  1.93 us

profile of v3, /device:TPU:1, one launch (start us, length us, event | category | flops | bytes accessed | tf_op | source)
XLA Modules:
  0.0 87.4 jit_solution(8763737492980590613)
XLA Ops:
  0.0 0.0 copy-start
  0.0 1.2 %copy-done = bf16[1,2,512,512]{3,2,1,0:T(8,128)(2,1)S(1)} copy-done((bf16[1,2,512,512]{3,2,1,0:T(8,128)(2,1)S(1)}, bf16[1,2,512,512]{3,2,1,0:T(8,128)(2,1)}, u32[]{:S(2)}) %copy-start) | copy-done | bytes 1048600
  1.2 0.0 copy-start.3
  1.2 0.7 copy-done.3
  1.9 2.4 %gram.1 = bf16[16,160,128]{2,1,0:T(8,128)(2,1)S(1)} custom-call(s32[2,2]{1,0:T(2,128)S(1)} %copy-done.3, bf16[1,2,512,512]{3,2,1,0:T(8,128)(2,1)S(1)} %copy-done), custom_call_target="tpu_custom_call" | custom-call | tf_op jit(solution)/shard_map/gram/pallas_call | solution.py:344
  4.3 0.0 copy-start.1
  4.3 0.0 copy-start.2
  4.3 0.0 copy-start.4
  4.3 0.0 copy-start.5
  4.3 0.0 copy-start.6
  4.4 18.5 %all_to_all.20.parts = bf16[16,160,128]{2,1,0:T(8,128)(2,1)S(1)} all-to-all(bf16[16,160,128]{2,1,0:T(8,128)(2,1)S(1)} %gram.1), channel_id=1, replica_groups=mesh['z'=4,'y'=4,'x'=4,'h'=4,'c'=2] {'y','x'}, dimensions={0} | all-to-all | bytes 1310720 | tf_op jit(solution)/shard_map/all_to_all | solution.py:353
  22.9 0.6 plane_sum.1
  23.4 12.0 %all_to_all.21.parts = bf16[4,160,128]{2,1,0:T(8,128)(2,1)S(1)} all-to-all(bf16[4,160,128]{2,1,0:T(8,128)(2,1)S(1)} %plane_sum.1), channel_id=1, replica_groups=mesh['z'=4,'y'=4,'x'=4,'h'=4,'c'=2] {'z'}, dimensions={0} | all-to-all | bytes 327680 | tf_op jit(solution)/shard_map/all_to_all | solution.py:357
  35.5 0.3 line_sum.1
  35.8 12.4 %all_to_all.22.packed = bf16[16,144,128]{2,1,0:T(8,128)(2,1)S(1)} all-to-all(bf16[16,144,128]{2,1,0:T(8,128)(2,1)S(1)} %get-tuple-element.9), channel_id=1, replica_groups=mesh['z'=4,'y'=4,'x'=4,'h'=4,'c'=2] {'y','x'}, dimensions={0} | all-to-all | bytes 1179648 | tf_op jit(solution)/shard_map/all_to_all | solution.py:366
  48.1 0.0 copy-done.1
  48.1 0.0 copy-done.2
  48.1 0.0 copy-done.4
  48.2 0.0 copy-done.5
  48.2 0.0 copy-done.6
  48.2 8.7 %roots_and_update.1 = (f32[2,512,512]{2,1,0:T(8,128)S(1)}, f32[8,8,128]{2,1,0:T(8,128)S(1)}) custom-call(s32[2,2]{1,0:T(2,128)S(1)} %copy-done.4, s32[2]{0:T(128)S(1)} %copy-done.5, f32[4]{0:T(128)S(1)} %copy-done.6, bf16[16,144,128]{2,1,0:T(8,128)(2,1)S(1)} %all_to_all.22.packed, f32[2,4,128]{2,1,0:T(4,128)S(1)} %get-tuple-element.10.diags, ...), custom_call_target="tpu_custom_call" | custom-call | tf_op jit(solution)/shard_map/roots_and_update/pallas_call | solution.py:367
  56.9 28.8 %all_to_all.23.sums = f32[8,8,128]{2,1,0:T(8,128)S(1)} all-to-all(f32[8,8,128]{2,1,0:T(8,128)S(1)} %get-tuple-element.11), channel_id=1, replica_groups=mesh['z'=4,'y'=4,'x'=4,'h'=4,'c'=2] {'h','c'}, dimensions={0} | all-to-all | bytes 65536 | tf_op jit(solution)/shard_map/all_to_all | solution.py:389
  85.7 1.7 %graft.1 = bf16[1,2,512,512]{3,2,1,0:T(8,128)(2,1)} custom-call(s32[2]{0:T(128)S(1)} %copy-done.5, f32[8,8,128]{2,1,0:T(8,128)S(1)} %all_to_all.23.sums, f32[2,512,512]{2,1,0:T(8,128)S(1)} %get-tuple-element.12.update), custom_call_target="tpu_custom_call" | custom-call | tf_op jit(solution)/shard_map/graft/pallas_call | solution.py:390
Async XLA Ops:
  0.0 1.2 %copy-start = (bf16[1,2,512,512]{3,2,1,0:T(8,128)(2,1)S(1)}, bf16[1,2,512,512]{3,2,1,0:T(8,128)(2,1)}, u32[]{:S(2)}) copy-start(bf16[1,2,512,512]{3,2,1,0:T(8,128)(2,1)} %g_hbm.1) | copy-start | bytes 3145732
  1.2 0.7 copy-start.3
  4.3 43.9 %copy-start.1 = (bf16[1,2,512,512]{3,2,1,0:T(8,128)(2,1)S(1)}, bf16[1,2,512,512]{3,2,1,0:T(8,128)(2,1)}, u32[]{:S(2)}) copy-start(bf16[1,2,512,512]{3,2,1,0:T(8,128)(2,1)} %g_hbm.1) | copy-start | bytes 3145732
  4.3 43.8 %copy-start.2 = (bf16[2,2,512,512]{3,2,1,0:T(8,128)(2,1)S(1)}, bf16[2,2,512,512]{3,2,1,0:T(8,128)(2,1)}, u32[]{:S(2)}) copy-start(bf16[2,2,512,512]{3,2,1,0:T(8,128)(2,1)} %param.6) | copy-start | bytes 6291460
  4.3 43.8 %copy-start.4 = (s32[2,2]{1,0:T(2,128)S(1)}, s32[2,2]{1,0:T(2,128)}, u32[]{:S(2)}) copy-start(s32[2,2]{1,0:T(2,128)} %owners.3) | copy-start | bytes 52
  4.3 43.8 %copy-start.5 = (s32[2]{0:T(128)S(1)}, s32[2]{0:T(128)}, u32[]{:S(2)}) copy-start(s32[2]{0:T(128)} %layers.3) | copy-start | bytes 28
  4.3 43.8 %copy-start.6 = (f32[4]{0:T(128)S(1)}, f32[4]{0:T(128)}, u32[]{:S(2)}) copy-start(f32[4]{0:T(128)} %damping.1) | copy-start | bytes 52

commit v4 on v3

--- a/solution.py
+++ b/solution.py
@@ -17,11 +17,12 @@
 CHUNKS = 16
 ROWS = B // CHUNKS
 SPAN = 240.0
+PIECES = 2
 TINY = 1e-30
 f32, bf16 = jnp.float32, jnp.bfloat16
 VMEM = pl.BlockSpec(memory_space=pltpu.VMEM)
 SMEM = pl.BlockSpec(memory_space=pltpu.SMEM)
-ANY = pl.BlockSpec(memory_space=pl.ANY)
+ANY = pl.BlockSpec(memory_space=pltpu.HBM)
 
 
 def params(mib):
@@ -70,8 +71,15 @@
     return tail[0:4] + tail[4:8] + tail[8:12], tail[12:13] * (1.0 / SPAN)
 
 
-def gram_kernel(owners, g_hbm, out, g, grams, flip, sems):
-    copies = [pltpu.make_async_copy(g_hbm.at[0, b], g.at[b], sems.at[b]) for b in range(NB)]
+def kind(k, j):
+    if k * ROWS > j * T + T - 1:
+        return 1
+    return -1 if k * ROWS + ROWS - 1 < j * T else 0
+
+
+def gram_kernel(owners_hbm, g_hbm, out, owners, g, grams, flip, sems):
+    copies = [pltpu.make_async_copy(owners_hbm, owners, sems.at[NB])]
+    copies += [pltpu.make_async_copy(g_hbm.at[0, b], g.at[b], sems.at[b]) for b in range(NB)]
     for c in copies:
         c.start()
     for c in copies:
@@ -88,34 +96,39 @@
             flip[...] = block.T
             grams[slot] = dot(flip[...], block)
 
-    row = lax.broadcasted_iota(jnp.int32, (ROWS, B), 0)
-    col = lax.broadcasted_iota(jnp.int32, (ROWS, B), 1)
-    diag = [jnp.zeros((1, B), f32), jnp.zeros((1, B), f32)]
-    most = [jnp.zeros((ROWS, B), f32), jnp.zeros((ROWS, B), f32)]
+    row = lax.broadcasted_iota(jnp.int32, (ROWS, T), 0)
+    col = lax.broadcasted_iota(jnp.int32, (ROWS, T), 1)
+    most = [jnp.zeros((ROWS, T), f32), jnp.zeros((ROWS, T), f32)]
+    diag = [[jnp.zeros((1, T), f32) for _ in range(NT)] for _ in range(2)]
     for k in range(CHUNKS):
         rows = slice(k * ROWS, (k + 1) * ROWS)
-        a, b = grams[0, rows, :], grams[1, rows, :]
-        on = row + k * ROWS == col
-        lower = row + k * ROWS > col
-        upper = row + k * ROWS < col
-        diag[0] = diag[0] + jnp.sum(jnp.where(on, a, 0.0), axis=0, keepdims=True)
-        diag[1] = diag[1] + jnp.sum(jnp.where(on, b, 0.0), axis=0, keepdims=True)
-        most[0] = jnp.maximum(most[0], jnp.where(lower, jnp.abs(a), 0.0))
-        most[1] = jnp.maximum(most[1], jnp.where(upper, jnp.abs(b), 0.0))
+        for j in range(NT):
+            cols = slice(j * T, (j + 1) * T)
+            where = kind(k, j)
+            if where:
+                s = (1 - where) // 2
+                most[s] = jnp.maximum(most[s], jnp.abs(grams[s, rows, cols]))
+            else:
+                gap = row - col + (k * ROWS - j * T)
+                for s in range(2):
+                    x = grams[s, rows, cols]
+                    diag[s][j] = diag[s][j] + jnp.sum(jnp.where(gap == 0, x, 0.0), axis=0, keepdims=True)
+                    most[s] = jnp.maximum(most[s], jnp.where(gap > 0 if s == 0 else gap < 0, jnp.abs(x), 0.0))
     tops = [top_of(m) for m in most]
     gains = [SPAN / t for t in tops]
+    tails = [tail_of(jnp.concatenate(diag[s], axis=0), tops[s]) for s in range(2)]
     for k in range(CHUNKS):
         rows = slice(k * ROWS, (k + 1) * ROWS)
-        lower = row + k * ROWS >= col
-        c = jnp.where(lower, grams[0, rows, :], grams[1, rows, :])
-        c = encode(c, jnp.where(lower, gains[0], gains[1]))
         for j in range(NT):
-            out[k, j * ROWS : (j + 1) * ROWS, :] = c[:, j * T : (j + 1) * T]
-    tails = []
-    for s in range(2):
-        d = jnp.concatenate([diag[s][:, j * T : (j + 1) * T] for j in range(NT)], axis=0)
-        tails.append(tail_of(d, tops[s]))
-    for k in range(CHUNKS):
+            cols = slice(j * T, (j + 1) * T)
+            where = kind(k, j)
+            if where:
+                s = (1 - where) // 2
+                code = encode(grams[s, rows, cols], gains[s])
+            else:
+                lower = row + k * ROWS >= col + j * T
+                code = encode(jnp.where(lower, grams[0, rows, cols], grams[1, rows, cols]), jnp.where(lower, gains[0], gains[1]))
+            out[k, j * ROWS : (j + 1) * ROWS, :] = code
         out[k, T : T + 16, :] = tails[0]
         out[k, T + 16 : T + 32, :] = tails[1]
 
@@ -178,14 +191,18 @@
         return Diag([f(c) for c in self.cols], [f(r) for r in self.rows])
 
 
-def main_kernel(owners, layers, damping, packed, diags, g, prev, update, sums, c_ref, x_ref, xo, s_ref, so, f_ref, fo, h_ref, ho, roots, accs, sem):
-    fetch = pltpu.make_async_copy(prev, roots, sem)
-    fetch.start()
+def main_kernel(owners_hbm, layers_hbm, damping_hbm, packed, diags, g, prev, update, sums, hot, owners, layers, damping, sems, c_ref, x_ref, xo, s_ref, so, f_ref, fo, h_ref, ho, roots, accs):
+    copies = [
+        pltpu.make_async_copy(owners_hbm, owners, sems.at[0]),
+        pltpu.make_async_copy(layers_hbm, layers, sems.at[1]),
+        pltpu.make_async_copy(damping_hbm, damping, sems.at[2]),
+    ]
+    for c in copies:
+        c.start()
     row = lax.broadcasted_iota(jnp.int32, (T, T), 0)
     col = lax.broadcasted_iota(jnp.int32, (T, T), 1)
     mask = row == col
     lower = row > col
-    ids = refreshed(owners)
     crow = lax.broadcasted_iota(jnp.int32, (ROWS, T), 0)
     ccol = lax.broadcasted_iota(jnp.int32, (ROWS, T), 1)
     squares = [jnp.zeros((ROWS, T), f32), jnp.zeros((ROWS, T), f32)]
@@ -209,6 +226,15 @@
                 squares[0] = squares[0] + jnp.where(r > c, q, 0.0)
                 squares[1] = squares[1] + jnp.where(r > c, 0.0, q)
             c_ref[k * ROWS : (k + 1) * ROWS, j * T : (j + 1) * T] = x
+
+    for c in copies:
+        c.wait()
+    ids = refreshed(owners)
+    for n in range(2 * NB):
+
+        @pl.when((ids[0] != n) & (ids[1] != n))
+        def _():
+            roots[n] = prev[n]
 
     def total(v):
         return jnp.sum(jnp.sum(v, axis=0, keepdims=True), axis=1, keepdims=True)
@@ -244,10 +270,9 @@
                     x_ref[s, 0, b[0], b[1]] = x
                     xo[s, 0, b[0], b[1]] = x.astype(bf16)
 
-    def finish(acc, off, da, db, keep):
-        diag = Diag([], [])
-        for i in range(NT):
-            for j in range(NT):
+    def finish(acc, off, da, db, keep, diag):
+        for j in range(NT):
+            for i in range(NT if j >= NT // 2 else NT // 2):
                 r, c = tile(i, j)
                 base = acc[r, c]
                 if i == j:
@@ -256,8 +281,24 @@
                     diag.rows.append(jnp.sum(on, axis=0, keepdims=True) + da.rows[i] * db.rows[i])
                     keep(r, c, jnp.where(mask, 0.0, base + off(i, j, r, c)), diag.rows[i])
                 else:
-                    keep(r, c, base + off(i, j, r, c), None)
-        return diag
+                    x = base + off(i, j, r, c)
+                    keep(r, c, x, None)
+                    if j >= NT // 2 and i < NT // 2:
+                        keep(c, r, x.T, None)
+            if j % 2:
+                yield
+
+    def product(acc, a, b):
+        left, right = slice(0, B // 2), slice(B // 2, B)
+        acc[left, left] = dot(a[left, :], b[:, left])
+        yield
+        acc[:, right] = dot(a[...], b[:, right])
+        yield
+
+    def together(*steps):
+        steps = list(steps)
+        while steps:
+            steps = [st for st in steps if next(st, steps) is not steps]
 
     def square_off(d, ref):
         return lambda i, j, r, c: ref[r, c] * (d.cols[i] + d.rows[j])
@@ -272,43 +313,50 @@
 
         return keep
 
-    first = dx
-    for it in range(2):
-        ds, df = [None, None], [None, None]
-        for s in range(2):
-            accs[s] = dot(xo[s, it], xo[s, it])
-            ds[s] = finish(accs.at[s], square_off(dx[s], x_ref.at[s, it]), dx[s], dx[s], keep_in(s_ref.at[s], so.at[s]))
-        for s in range(2):
-            accs[s] = dot(so[s], so[s])
-            df[s] = finish(accs.at[s], square_off(ds[s], s_ref.at[s]), ds[s], ds[s], keep_in(f_ref.at[s], fo.at[s]))
-        new = [None, None]
-        for s in range(2):
-            accs[s] = dot(fo[s], xo[s, it])
-            dy = dx[s].map(lambda v: v - 1.25)
-            new[s] = finish(
-                accs.at[s], cross_off(df[s], f_ref.at[s], dy, x_ref.at[s, it]), df[s], dy, keep_in(x_ref.at[s, it + 1], xo.at[s, it + 1])
-            ).map(lambda v: v + 1.25)
-        dx = new
-        if it == 0:
-            dh = [None, None]
-            for s in range(2):
-                accs[s] = dot(xo[s, 0], xo[s, 1])
-                dh[s] = finish(
-                    accs.at[s], cross_off(first[s], x_ref.at[s, 0], dx[s], x_ref.at[s, 1]), first[s], dx[s], keep_in(h_ref.at[s], ho.at[s])
+    def newton(s):
+        x = [dx[s]]
+        for it in range(2):
+            d = x[it]
+            ds, df, dn = Diag([], []), Diag([], []), Diag([], [])
+            yield product(accs.at[s], xo.at[s, it], xo.at[s, it]), finish(accs.at[s], square_off(d, x_ref.at[s, it]), d, d, keep_in(s_ref.at[s], so.at[s]), ds)
+            yield product(accs.at[s], so.at[s], so.at[s]), finish(accs.at[s], square_off(ds, s_ref.at[s]), ds, ds, keep_in(f_ref.at[s], fo.at[s]), df)
+            dy = d.map(lambda v: v - 1.25)
+            yield (
+                product(accs.at[s], fo.at[s], xo.at[s, it]),
+                finish(accs.at[s], cross_off(df, f_ref.at[s], dy, x_ref.at[s, it]), df, dy, keep_in(x_ref.at[s, it + 1], xo.at[s, it + 1]), dn),
+            )
+            x.append(dn.map(lambda v: v + 1.25))
+            if it == 0:
+                dh = Diag([], [])
+                yield (
+                    product(accs.at[s], xo.at[s, 0], xo.at[s, 1]),
+                    finish(accs.at[s], cross_off(x[0], x_ref.at[s, 0], x[1], x_ref.at[s, 1]), x[0], x[1], keep_in(h_ref.at[s], ho.at[s]), dh),
                 )
-    fetch.wait()
-    for s in range(2):
-        accs[s] = dot(ho[s], xo[s, 2])
-
-        def keep(r, c, x, on, s=s):
+
+        def keep(r, c, v, on):
             if on is not None:
-                x = jnp.where(mask, on, x)
-            roots[ids[s], r, c] = (x * scales[s]).astype(bf16)
-
-        finish(accs.at[s], cross_off(dh[s], h_ref.at[s], dx[s], x_ref.at[s, 2]), dh[s], dx[s], keep)
+                v = jnp.where(mask, on, v)
+            roots[ids[s], r, c] = (v * scales[s]).astype(bf16)
+
+        yield (
+            product(accs.at[s], ho.at[s], xo.at[s, 2]),
+            finish(accs.at[s], cross_off(dh, h_ref.at[s], x[2], x_ref.at[s, 2]), dh, x[2], keep, Diag([], [])),
+        )
+
+    chains = [newton(0), newton(1)]
+    waiting = None
+    for turn in range(16):
+        work, rest = next(chains[turn % 2])
+        together(*([work] if waiting is None else [work, waiting]))
+        waiting = rest
+    together(waiting)
     lane = lax.broadcasted_iota(jnp.int32, (8, T), 1)
     line = lax.broadcasted_iota(jnp.int32, (8, T), 0)
     tail = jnp.zeros((8, T), f32)
+    ones = jnp.zeros((8, T), f32)
+    for b in range(NB):
+        ones = jnp.where((lane == layers[b]) & (line == b), 1.0, ones)
+    hot[...] = ones
     for b in range(NB):
         half = dot(roots[2 * b], g[b]).astype(bf16)
         u = dot(half, roots[2 * b + 1])
@@ -320,42 +368,52 @@
         sums[k] = tail
 
 
-def scale_kernel(layers, sums, update, out, scaled, sems):
+def scale_kernel(hot, sums, update, out, scaled, sems):
     total = sums[0]
     for k in range(1, sums.shape[0]):
         total = total + sums[k]
     ratio = jnp.sqrt((total[0:1] + NORM_EPSILON) / (total[1:2] + NORM_EPSILON))
-    lane = lax.broadcasted_iota(jnp.int32, (1, T), 1)
     copies = []
     for b in range(NB):
-        mine = jnp.sum(jnp.where(lane == layers[b], ratio, 0.0), axis=1, keepdims=True)
-        for h in range(2):
-            rows = pl.ds(h * (B // 2), B // 2)
+        mine = jnp.sum(hot[b : b + 1] * ratio, axis=1, keepdims=True)
+        for h in range(PIECES):
+            rows = pl.ds(h * (B // PIECES), B // PIECES)
             scaled[b, rows, :] = (update[b, rows, :] * mine).astype(bf16)
-            copies.append(pltpu.make_async_copy(scaled.at[b, rows], out.at[0, b, rows], sems.at[2 * b + h]))
+            copies.append(pltpu.make_async_copy(scaled.at[b, rows], out.at[0, b, rows], sems.at[b, h]))
             copies[-1].start()
     for c in copies:
         c.wait()
 
 
-def per_device(grads, prev_roots, damping, block_layer, owners):
-    prev = prev_roots.reshape(2 * NB, B, B)
-    shape = jax.ShapeDtypeStruct
-    packed = pl.pallas_call(
+shape = jax.ShapeDtypeStruct
+
+
+def gram_call(owners, grads):
+    return pl.pallas_call(
         gram_kernel,
         out_shape=shape((CHUNKS, T + 32, T), bf16),
-        in_specs=[SMEM, ANY],
+        in_specs=[ANY, ANY],
         out_specs=VMEM,
-        scratch_shapes=[pltpu.VMEM((NB, B, B), bf16), pltpu.VMEM((2, B, B), f32), pltpu.VMEM((B, B), bf16), pltpu.SemaphoreType.DMA((NB,))],
-        compiler_params=params(16),
+        scratch_shapes=[
+            pltpu.SMEM((NB, 2), jnp.int32),
+            pltpu.VMEM((NB, B, B), bf16),
+            pltpu.VMEM((2, B, B), f32),
+            pltpu.VMEM((B, B), bf16),
+            pltpu.SemaphoreType.DMA((NB + 1,)),
+        ],
+        compiler_params=params(53),
         name="gram",
     )(owners, grads)
-    packed = lax.all_to_all(packed, PLANE, 0, 0)
-    packed = pl.pallas_call(
+
+
+def plane_call(packed):
+    return pl.pallas_call(
         plane_sum_kernel, out_shape=shape((4, T + 32, T), bf16), in_specs=[VMEM], out_specs=VMEM, compiler_params=params(16), name="plane_sum"
     )(packed)
-    packed = lax.all_to_all(packed, "z", 0, 0)
-    packed, diags = pl.pallas_call(
+
+
+def line_call(packed):
+    return pl.pallas_call(
         line_sum_kernel,
         out_shape=[shape((CHUNKS, T + 16, T), bf16), shape((2, 4, T), f32)],
         in_specs=[VMEM],
@@ -363,13 +421,19 @@
         compiler_params=params(16),
         name="line_sum",
     )(packed)
-    packed = lax.all_to_all(packed, PLANE, 0, 0)
-    update, sums = pl.pallas_call(
+
+
+def roots_call(owners, block_layer, damping, packed, diags, grads, prev):
+    return pl.pallas_call(
         main_kernel,
-        out_shape=[shape((NB, B, B), f32), shape((8, 8, T), f32)],
-        in_specs=[SMEM, SMEM, SMEM, VMEM, VMEM, VMEM, ANY],
-        out_specs=[VMEM, VMEM],
+        out_shape=[shape((NB, B, B), f32), shape((8, 8, T), f32), shape((8, T), f32)],
+        in_specs=[ANY, ANY, ANY, VMEM, VMEM, VMEM, VMEM],
+        out_specs=[VMEM, VMEM, VMEM],
         scratch_shapes=[
+            pltpu.SMEM((NB, 2), jnp.int32),
+            pltpu.SMEM((NB,), jnp.int32),
+            pltpu.SMEM((LAYERS,), f32),
+            pltpu.SemaphoreType.DMA((3,)),
             pltpu.VMEM((B, B), f32),
             pltpu.VMEM((2, 3, B, B), f32),
             pltpu.VMEM((2, 3, B, B), bf16),
@@ -381,21 +445,31 @@
             pltpu.VMEM((2, B, B), bf16),
             pltpu.VMEM((4, B, B), bf16),
             pltpu.VMEM((2, B, B), f32),
-            pltpu.SemaphoreType.DMA,
         ],
         compiler_params=params(40),
         name="roots_and_update",
     )(owners, block_layer, damping, packed, diags, grads[0], prev)
-    sums = lax.all_to_all(sums, COLUMN, 0, 0)
+
+
+def graft_call(hot, sums, update):
     return pl.pallas_call(
         scale_kernel,
         out_shape=shape((1, NB, B, B), bf16),
-        in_specs=[SMEM, VMEM, VMEM],
+        in_specs=[VMEM, VMEM, VMEM],
         out_specs=ANY,
-        scratch_shapes=[pltpu.VMEM((NB, B, B), bf16), pltpu.SemaphoreType.DMA((2 * NB,))],
+        scratch_shapes=[pltpu.VMEM((NB, B, B), bf16), pltpu.SemaphoreType.DMA((NB, PIECES))],
         compiler_params=params(16),
         name="graft",
-    )(block_layer, sums, update)
+    )(hot, sums, update)
+
+
+def per_device(grads, prev_roots, damping, block_layer, owners):
+    packed = lax.all_to_all(gram_call(owners, grads), PLANE, 0, 0)
+    packed = lax.all_to_all(plane_call(packed), "z", 0, 0)
+    packed, diags = line_call(packed)
+    packed = lax.all_to_all(packed, PLANE, 0, 0)
+    update, sums, hot = roots_call(owners, block_layer, damping, packed, diags, grads, prev_roots.reshape(2 * NB, B, B))
+    return graft_call(hot, lax.all_to_all(sums, COLUMN, 0, 0), update)
 
 
 def solution(mesh):

time: 87.7 us -> 85.3 us (0.973)
  local copies, waits for them, and re-layouts: 1.93 us -> 0.7 us
  Pallas kernels: 13.6 us -> 12.5 us
    all_to_all x2 -> x3, blocking collectives: 40.9 us -> 59.4 us  [the longest x1 28.8 us: per_device(): return graft_call(hot, lax.all_to_all(sums, COLUMN, 0, 0), update)]
    all_to_all x2 -> x1, blocking collectives: 30.9 us -> 12.4 us  [per_device(): packed = lax.all_to_all(packed, PLANE, 0, 0)]
    unnamed x14 -> x10, local copies, waits for them, and re-layouts: 1.93 us -> 0.7 us
    pallas_call x5, Pallas kernels: 13.6 us -> 12.5 us  [the longest x1 7.59 us: roots_call(): pl.pallas_call(main_kernel, out_shape=[shape((NB, B, B), f32), shape((8,...]
where the time goes in v4:
time: 85.3 us; the launch traced here: 85 us
  blocking collectives  71.7 us (84%)
  Pallas kernels  12.5 us (15%)
    all_to_all x1, blocking collectives, per_device(): return graft_call(hot, lax.all_to_all(sums, COLUMN, 0, 0), update)  28.8 us
    all_to_all x1, blocking collectives, per_device(): packed = lax.all_to_all(gram_call(owners, grads), PLANE, 0, 0)  18.5 us
    all_to_all x1, blocking collectives, per_device(): packed = lax.all_to_all(packed, PLANE, 0, 0)  12.4 us
    all_to_all x1, blocking collectives, per_device(): packed = lax.all_to_all(plane_call(packed), 'z', 0, 0)  12 us
    pallas_call x1, Pallas kernels, roots_call(): pl.pallas_call(main_kernel, out_shape=[shape((NB, B, B), f32), shape((8,...  7.59 us
    pallas_call x1, Pallas kernels, gram_call(): pl.pallas_call(gram_kernel, out_shape=shape((CHUNKS, T + 32, T), bf16), i...  2.87 us

profile of v4, /device:TPU:1, one launch (start us, length us, event | category | flops | bytes accessed | tf_op | source)
XLA Modules:
  0.0 85.0 jit_solution(6568924913642105658)
XLA Ops:
  0.0 0.0 copy-start.2
  0.0 0.7 copy-done.2
  0.7 2.9 %gram.1 = bf16[16,160,128]{2,1,0:T(8,128)(2,1)S(1)} custom-call(s32[2,2]{1,0:T(2,128)S(1)} %copy-done.2, bf16[1,2,512,512]{3,2,1,0:T(8,128)(2,1)} %g_hbm.1), custom_call_target="tpu_custom_call" | custom-call | tf_op jit(solution)/shard_map/gram/pallas_call | solution.py:392
  3.6 0.0 copy-start
  3.6 0.0 copy-start.1
  3.6 0.0 copy-start.3
  3.6 0.0 copy-start.4
  3.6 18.5 %all_to_all.20.parts = bf16[16,160,128]{2,1,0:T(8,128)(2,1)S(1)} all-to-all(bf16[16,160,128]{2,1,0:T(8,128)(2,1)S(1)} %gram.1), channel_id=1, replica_groups=mesh['z'=4,'y'=4,'x'=4,'h'=4,'c'=2] {'y','x'}, dimensions={0} | all-to-all | bytes 1310720 | tf_op jit(solution)/shard_map/all_to_all | solution.py:467
  22.1 0.6 plane_sum.1
  22.7 12.0 %all_to_all.21.parts = bf16[4,160,128]{2,1,0:T(8,128)(2,1)S(1)} all-to-all(bf16[4,160,128]{2,1,0:T(8,128)(2,1)S(1)} %plane_sum.1), channel_id=1, replica_groups=mesh['z'=4,'y'=4,'x'=4,'h'=4,'c'=2] {'z'}, dimensions={0} | all-to-all | bytes 327680 | tf_op jit(solution)/shard_map/all_to_all | solution.py:468
  34.7 0.3 line_sum.1
  35.0 12.4 %all_to_all.22.packed = bf16[16,144,128]{2,1,0:T(8,128)(2,1)S(1)} all-to-all(bf16[16,144,128]{2,1,0:T(8,128)(2,1)S(1)} %get-tuple-element.10), channel_id=1, replica_groups=mesh['z'=4,'y'=4,'x'=4,'h'=4,'c'=2] {'y','x'}, dimensions={0} | all-to-all | bytes 1179648 | tf_op jit(solution)/shard_map/all_to_all | solution.py:470
  47.4 0.0 copy-done
  47.4 0.0 copy-done.1
  47.4 0.0 copy-done.3
  47.4 0.0 copy-done.4
  47.4 7.6 %roots_and_update.1 = (f32[2,512,512]{2,1,0:T(8,128)S(1)}, f32[8,8,128]{2,1,0:T(8,128)S(1)}, f32[8,128]{1,0:T(8,128)S(1)}) custom-call(s32[2,2]{1,0:T(2,128)S(1)} %copy-done.2, s32[2]{0:T(128)S(1)} %copy-done.3, f32[4]{0:T(128)S(1)} %copy-done.4, bf16[16,144,128]{2,1,0:T(8,128)(2,1)S(1)} %all_to_all.22.packed, f32[2,4,128]{2,1,0:T(4,128)S(1)} %get-tuple-element.11.diags, ...), custom_call_target="tpu_custom_call" | custom-call | tf_op jit(solution)/shard_map/roots_and_update/pallas_call | solution.py:427
  55.0 28.8 %all_to_all.23.sums = f32[8,8,128]{2,1,0:T(8,128)S(1)} all-to-all(f32[8,8,128]{2,1,0:T(8,128)S(1)} %get-tuple-element.13), channel_id=1, replica_groups=mesh['z'=4,'y'=4,'x'=4,'h'=4,'c'=2] {'h','c'}, dimensions={0} | all-to-all | bytes 65536 | tf_op jit(solution)/shard_map/all_to_all | solution.py:472
  83.9 1.1 %graft.1 = bf16[1,2,512,512]{3,2,1,0:T(8,128)(2,1)} custom-call(f32[8,128]{1,0:T(8,128)S(1)} %get-tuple-element.12.hot, f32[8,8,128]{2,1,0:T(8,128)S(1)} %all_to_all.23.sums, f32[2,512,512]{2,1,0:T(8,128)S(1)} %get-tuple-element.14.update), custom_call_target="tpu_custom_call" | custom-call | tf_op jit(solution)/shard_map/graft/pallas_call | solution.py:455
Async XLA Ops:
  0.0 0.7 copy-start.2
  3.6 43.9 %copy-start = (bf16[1,2,512,512]{3,2,1,0:T(8,128)(2,1)S(1)}, bf16[1,2,512,512]{3,2,1,0:T(8,128)(2,1)}, u32[]{:S(2)}) copy-start(bf16[1,2,512,512]{3,2,1,0:T(8,128)(2,1)} %g_hbm.1) | copy-start | bytes 3145732
  3.6 43.9 %copy-start.1 = (bf16[2,2,512,512]{3,2,1,0:T(8,128)(2,1)S(1)}, bf16[2,2,512,512]{3,2,1,0:T(8,128)(2,1)}, u32[]{:S(2)}) copy-start(bf16[2,2,512,512]{3,2,1,0:T(8,128)(2,1)} %param.6) | copy-start | bytes 6291460
  3.6 43.9 %copy-start.3 = (s32[2]{0:T(128)S(1)}, s32[2]{0:T(128)}, u32[]{:S(2)}) copy-start(s32[2]{0:T(128)} %layers_hbm.1) | copy-start | bytes 28
  3.6 43.8 %copy-start.4 = (f32[4]{0:T(128)S(1)}, f32[4]{0:T(128)}, u32[]{:S(2)}) copy-start(f32[4]{0:T(128)} %damping_hbm.1) | copy-start | bytes 52

commit v5 on v4

--- a/solution.py
+++ b/solution.py
@@ -1,3 +1,5 @@
+import math
+
 import jax
 import jax.numpy as jnp
 from jax import lax
@@ -17,7 +19,10 @@
 CHUNKS = 16
 ROWS = B // CHUNKS
 SPAN = 240.0
+HALF = SPAN / 2 * math.log(2.0)
+UNIT = 1.0 / (SPAN * math.log(2.0))
 PIECES = 2
+TAIL = 16
 TINY = 1e-30
 f32, bf16 = jnp.float32, jnp.bfloat16
 VMEM = pl.BlockSpec(memory_space=pltpu.VMEM)
@@ -52,7 +57,7 @@
 
 def decode(code, top):
     code = code.astype(f32)
-    size = (jnp.log2(jnp.abs(code)) + SPAN / 2) * top
+    size = (jnp.log(jnp.abs(code)) + HALF) * top
     return jnp.where(code < 0, -size, size)
 
 
@@ -62,13 +67,14 @@
     return [hi, mid, x - hi - mid]
 
 
-def tail_of(diag, top):
-    return jnp.concatenate(parts3(diag) + [jnp.broadcast_to(top, (4, T))], axis=0).astype(bf16)
+def tail_of(diags, tops):
+    rows = parts3(diags[0]) + parts3(diags[1]) + [jnp.broadcast_to(t, (1, T)) for t in tops]
+    return jnp.concatenate(rows + [jnp.zeros((8, T), f32)], axis=0).astype(bf16)
 
 
 def read_tail(tail):
-    tail = tail.astype(f32)
-    return tail[0:4] + tail[4:8] + tail[8:12], tail[12:13] * (1.0 / SPAN)
+    t = tail.astype(f32)
+    return [t[0:1] + t[1:2] + t[2:3], t[3:4] + t[4:5] + t[5:6]], [t[6:7] * UNIT, t[7:8] * UNIT]
 
 
 def kind(k, j):
@@ -116,7 +122,7 @@
                     most[s] = jnp.maximum(most[s], jnp.where(gap > 0 if s == 0 else gap < 0, jnp.abs(x), 0.0))
     tops = [top_of(m) for m in most]
     gains = [SPAN / t for t in tops]
-    tails = [tail_of(jnp.concatenate(diag[s], axis=0), tops[s]) for s in range(2)]
+    tails = [tail_of([diag[0][j], diag[1][j]], tops) for j in range(NT)]
     for k in range(CHUNKS):
         rows = slice(k * ROWS, (k + 1) * ROWS)
         for j in range(NT):
@@ -129,8 +135,7 @@
                 lower = row + k * ROWS >= col + j * T
                 code = encode(jnp.where(lower, grams[0, rows, cols], grams[1, rows, cols]), jnp.where(lower, gains[0], gains[1]))
             out[k, j * ROWS : (j + 1) * ROWS, :] = code
-        out[k, T : T + 16, :] = tails[0]
-        out[k, T + 16 : T + 32, :] = tails[1]
+        out[k, T : T + TAIL, :] = tails[k * ROWS // T]
 
 
 def chunk_place():
@@ -141,12 +146,11 @@
 
 def add_parts(parts, lower):
     total = jnp.zeros((T, T), f32)
-    diag = [jnp.zeros((4, T), f32), jnp.zeros((4, T), f32)]
+    diag = [jnp.zeros((1, T), f32), jnp.zeros((1, T), f32)]
     for p in range(parts.shape[0]):
-        da, ta = read_tail(parts[p, T : T + 16, :])
-        db, tb = read_tail(parts[p, T + 16 : T + 32, :])
-        total = total + decode(parts[p, :T, :], jnp.where(lower, ta, tb))
-        diag = [diag[0] + da, diag[1] + db]
+        d, tops = read_tail(parts[p, T : T + TAIL, :])
+        total = total + decode(parts[p, :T, :], jnp.where(lower, tops[0], tops[1]))
+        diag = [diag[0] + d[0], diag[1] + d[1]]
     return total, diag
 
 
@@ -155,28 +159,14 @@
     return encode(total, jnp.where(row >= col, SPAN / tops[0], SPAN / tops[1])), tops
 
 
-def plane_sum_kernel(parts, out):
+def sum_kernel(parts, out):
     row, col = chunk_place()
     total, diag = add_parts(parts, row >= col)
     code, tops = code_total(total, row, col)
-    tails = [tail_of(diag[s], tops[s]) for s in range(2)]
+    tail = tail_of(diag, tops)
     for k in range(out.shape[0]):
         out[k, :T, :] = code
-        out[k, T : T + 16, :] = tails[0]
-        out[k, T + 16 : T + 32, :] = tails[1]
-
-
-def line_sum_kernel(parts, out, diag_out):
-    row, col = chunk_place()
-    total, diag = add_parts(parts, row >= col)
-    code, tops = code_total(total, row, col)
-    diag_out[0] = diag[0]
-    diag_out[1] = diag[1]
-    line = lax.broadcasted_iota(jnp.int32, (16, T), 0)
-    tail = jnp.where(line < 8, tops[0], tops[1]).astype(bf16)
-    for k in range(out.shape[0]):
-        out[k, :T, :] = code
-        out[k, T : T + 16, :] = tail
+        out[k, T : T + TAIL, :] = tail
 
 
 def tile(i, j):
@@ -191,7 +181,7 @@
         return Diag([f(c) for c in self.cols], [f(r) for r in self.rows])
 
 
-def main_kernel(owners_hbm, layers_hbm, damping_hbm, packed, diags, g, prev, update, sums, hot, owners, layers, damping, sems, c_ref, x_ref, xo, s_ref, so, f_ref, fo, h_ref, ho, roots, accs):
+def main_kernel(owners_hbm, layers_hbm, damping_hbm, packed, g, prev, update, sums, hot, owners, layers, damping, sems, c_ref, x_ref, xo, s_ref, so, f_ref, fo, h_ref, ho, roots, accs):
     copies = [
         pltpu.make_async_copy(owners_hbm, owners, sems.at[0]),
         pltpu.make_async_copy(layers_hbm, layers, sems.at[1]),
@@ -206,9 +196,13 @@
     crow = lax.broadcasted_iota(jnp.int32, (ROWS, T), 0)
     ccol = lax.broadcasted_iota(jnp.int32, (ROWS, T), 1)
     squares = [jnp.zeros((ROWS, T), f32), jnp.zeros((ROWS, T), f32)]
+    diags = [[], []]
     for k in range(CHUNKS):
-        tail = packed[k, T : T + 16, :].astype(f32) * (1.0 / (SPAN * SHARDS * B))
-        ta, tb = tail[0:1], tail[8:9]
+        pieces, tops = read_tail(packed[k, T : T + TAIL, :])
+        ta, tb = [t * (1.0 / (SHARDS * B)) for t in tops]
+        if k * ROWS % T == 0:
+            for s in range(2):
+                diags[s].append(pieces[s] * (1.0 / (SHARDS * B)))
         for j in range(NT):
             code = packed[k, j * ROWS : (j + 1) * ROWS, :]
             low, high = k * ROWS - j * T - (T - 1), k * ROWS + ROWS - 1 - j * T
@@ -244,7 +238,7 @@
 
     dx, scales = [None, None], [None, None]
     for s in range(2):
-        d = diags[s] * (1.0 / (SHARDS * B))
+        d = jnp.concatenate(diags[s], axis=0)
         trace = total(d)
         shift = damping[layers[ids[s] // 2]] * trace * (1.0 / B)
         d = d + shift
@@ -391,7 +385,7 @@
 def gram_call(owners, grads):
     return pl.pallas_call(
         gram_kernel,
-        out_shape=shape((CHUNKS, T + 32, T), bf16),
+        out_shape=shape((CHUNKS, T + TAIL, T), bf16),
         in_specs=[ANY, ANY],
         out_specs=VMEM,
         scratch_shapes=[
@@ -406,28 +400,17 @@
     )(owners, grads)
 
 
-def plane_call(packed):
+def sum_call(packed, copies, name):
     return pl.pallas_call(
-        plane_sum_kernel, out_shape=shape((4, T + 32, T), bf16), in_specs=[VMEM], out_specs=VMEM, compiler_params=params(16), name="plane_sum"
+        sum_kernel, out_shape=shape((copies, T + TAIL, T), bf16), in_specs=[VMEM], out_specs=VMEM, compiler_params=params(16), name=name
     )(packed)
 
 
-def line_call(packed):
-    return pl.pallas_call(
-        line_sum_kernel,
-        out_shape=[shape((CHUNKS, T + 16, T), bf16), shape((2, 4, T), f32)],
-        in_specs=[VMEM],
-        out_specs=[VMEM, VMEM],
-        compiler_params=params(16),
-        name="line_sum",
-    )(packed)
-
-
-def roots_call(owners, block_layer, damping, packed, diags, grads, prev):
+def roots_call(owners, block_layer, damping, packed, grads, prev):
     return pl.pallas_call(
         main_kernel,
         out_shape=[shape((NB, B, B), f32), shape((8, 8, T), f32), shape((8, T), f32)],
-        in_specs=[ANY, ANY, ANY, VMEM, VMEM, VMEM, VMEM],
+        in_specs=[ANY, ANY, ANY, VMEM, VMEM, VMEM],
         out_specs=[VMEM, VMEM, VMEM],
         scratch_shapes=[
             pltpu.SMEM((NB, 2), jnp.int32),
@@ -448,7 +431,7 @@
         ],
         compiler_params=params(40),
         name="roots_and_update",
-    )(owners, block_layer, damping, packed, diags, grads[0], prev)
+    )(owners, block_layer, damping, packed, grads[0], prev)
 
 
 def graft_call(hot, sums, update):
@@ -465,10 +448,9 @@
 
 def per_device(grads, prev_roots, damping, block_layer, owners):
     packed = lax.all_to_all(gram_call(owners, grads), PLANE, 0, 0)
-    packed = lax.all_to_all(plane_call(packed), "z", 0, 0)
-    packed, diags = line_call(packed)
-    packed = lax.all_to_all(packed, PLANE, 0, 0)
-    update, sums, hot = roots_call(owners, block_layer, damping, packed, diags, grads, prev_roots.reshape(2 * NB, B, B))
+    packed = lax.all_to_all(sum_call(packed, 4, "plane_sum"), "z", 0, 0)
+    packed = lax.all_to_all(sum_call(packed, CHUNKS, "line_sum"), PLANE, 0, 0)
+    update, sums, hot = roots_call(owners, block_layer, damping, packed, grads, prev_roots.reshape(2 * NB, B, B))
     return graft_call(hot, lax.all_to_all(sums, COLUMN, 0, 0), update)
 
 

time: 85.3 us -> 84.7 us (level)
  no operation moved by 1% of the time
where the time goes in v5:
time: 84.7 us; the launch traced here: 84.4 us
  blocking collectives  71.1 us (84%)
  Pallas kernels  12.5 us (15%)
    all_to_all x1, blocking collectives, per_device(): return graft_call(hot, lax.all_to_all(sums, COLUMN, 0, 0), update)  28.9 us
    all_to_all x1, blocking collectives, per_device(): packed = lax.all_to_all(gram_call(owners, grads), PLANE, 0, 0)  17.9 us
    all_to_all x1, blocking collectives, per_device(): packed = lax.all_to_all(sum_call(packed, CHUNKS, 'line_sum'), PLANE, 0, 0)  12.3 us
    all_to_all x1, blocking collectives, per_device(): packed = lax.all_to_all(sum_call(packed, 4, 'plane_sum'), 'z', 0, 0)  12.1 us
    pallas_call x1, Pallas kernels, roots_call(): pl.pallas_call(main_kernel, out_shape=[shape((NB, B, B), f32), shape((8,...  7.59 us
    pallas_call x1, Pallas kernels, gram_call(): pl.pallas_call(gram_kernel, out_shape=shape((CHUNKS, T + TAIL, T), bf16),...  2.88 us

profile of v5, /device:TPU:1, one launch (start us, length us, event | category | flops | bytes accessed | tf_op | source)
XLA Modules:
  0.0 84.4 jit_solution(544103342238662454)
XLA Ops:
  0.0 0.0 copy-start.2
  0.0 0.7 copy-done.2
  0.7 2.9 %gram.1 = bf16[16,144,128]{2,1,0:T(8,128)(2,1)S(1)} custom-call(s32[2,2]{1,0:T(2,128)S(1)} %copy-done.2, bf16[1,2,512,512]{3,2,1,0:T(8,128)(2,1)} %g_hbm.1), custom_call_target="tpu_custom_call" | custom-call | tf_op jit(solution)/shard_map/gram/pallas_call | solution.py:386
  3.6 0.0 copy-start
  3.6 0.0 copy-start.1
  3.6 0.0 copy-start.3
  3.6 0.0 copy-start.4
  3.6 17.9 %all_to_all.20.parts = bf16[16,144,128]{2,1,0:T(8,128)(2,1)S(1)} all-to-all(bf16[16,144,128]{2,1,0:T(8,128)(2,1)S(1)} %gram.1), channel_id=1, replica_groups=mesh['z'=4,'y'=4,'x'=4,'h'=4,'c'=2] {'y','x'}, dimensions={0} | all-to-all | bytes 1179648 | tf_op jit(solution)/shard_map/all_to_all | solution.py:450
  21.5 0.6 plane_sum.1
  22.1 12.1 %all_to_all.21.parts = bf16[4,144,128]{2,1,0:T(8,128)(2,1)S(1)} all-to-all(bf16[4,144,128]{2,1,0:T(8,128)(2,1)S(1)} %plane_sum.1), channel_id=1, replica_groups=mesh['z'=4,'y'=4,'x'=4,'h'=4,'c'=2] {'z'}, dimensions={0} | all-to-all | bytes 294912 | tf_op jit(solution)/shard_map/all_to_all | solution.py:451
  34.2 0.3 line_sum.1
  34.5 12.3 %all_to_all.22.packed = bf16[16,144,128]{2,1,0:T(8,128)(2,1)S(1)} all-to-all(bf16[16,144,128]{2,1,0:T(8,128)(2,1)S(1)} %line_sum.1), channel_id=1, replica_groups=mesh['z'=4,'y'=4,'x'=4,'h'=4,'c'=2] {'y','x'}, dimensions={0} | all-to-all | bytes 1179648 | tf_op jit(solution)/shard_map/all_to_all | solution.py:452
  46.8 0.0 copy-done
  46.8 0.0 copy-done.1
  46.8 0.0 copy-done.3
  46.8 0.0 copy-done.4
  46.8 7.6 %roots_and_update.1 = (f32[2,512,512]{2,1,0:T(8,128)S(1)}, f32[8,8,128]{2,1,0:T(8,128)S(1)}, f32[8,128]{1,0:T(8,128)S(1)}) custom-call(s32[2,2]{1,0:T(2,128)S(1)} %copy-done.2, s32[2]{0:T(128)S(1)} %copy-done.3, f32[4]{0:T(128)S(1)} %copy-done.4, bf16[16,144,128]{2,1,0:T(8,128)(2,1)S(1)} %all_to_all.22.packed, bf16[2,512,512]{2,1,0:T(8,128)(2,1)S(1)} %bitcast.2, ...), custom_call_target="tpu_custom_call" | custom-call | tf_op jit(solution)/shard_map/roots_and_update/pallas_call | solution.py:410
  54.4 28.9 %all_to_all.23.sums = f32[8,8,128]{2,1,0:T(8,128)S(1)} all-to-all(f32[8,8,128]{2,1,0:T(8,128)S(1)} %get-tuple-element.9), channel_id=1, replica_groups=mesh['z'=4,'y'=4,'x'=4,'h'=4,'c'=2] {'h','c'}, dimensions={0} | all-to-all | bytes 65536 | tf_op jit(solution)/shard_map/all_to_all | solution.py:454
  83.3 1.1 %graft.1 = bf16[1,2,512,512]{3,2,1,0:T(8,128)(2,1)} custom-call(f32[8,128]{1,0:T(8,128)S(1)} %get-tuple-element.8.hot, f32[8,8,128]{2,1,0:T(8,128)S(1)} %all_to_all.23.sums, f32[2,512,512]{2,1,0:T(8,128)S(1)} %get-tuple-element.10.update), custom_call_target="tpu_custom_call" | custom-call | tf_op jit(solution)/shard_map/graft/pallas_call | solution.py:438
Async XLA Ops:
  0.0 0.7 copy-start.2
  3.6 43.2 %copy-start = (bf16[1,2,512,512]{3,2,1,0:T(8,128)(2,1)S(1)}, bf16[1,2,512,512]{3,2,1,0:T(8,128)(2,1)}, u32[]{:S(2)}) copy-start(bf16[1,2,512,512]{3,2,1,0:T(8,128)(2,1)} %g_hbm.1) | copy-start | bytes 3145732
  3.6 43.2 %copy-start.1 = (bf16[2,2,512,512]{3,2,1,0:T(8,128)(2,1)S(1)}, bf16[2,2,512,512]{3,2,1,0:T(8,128)(2,1)}, u32[]{:S(2)}) copy-start(bf16[2,2,512,512]{3,2,1,0:T(8,128)(2,1)} %param.6) | copy-start | bytes 6291460
  3.6 43.2 %copy-start.3 = (s32[2]{0:T(128)S(1)}, s32[2]{0:T(128)}, u32[]{:S(2)}) copy-start(s32[2]{0:T(128)} %layers_hbm.1) | copy-start | bytes 28
  3.6 43.2 %copy-start.4 = (f32[4]{0:T(128)S(1)}, f32[4]{0:T(128)}, u32[]{:S(2)}) copy-start(f32[4]{0:T(128)} %damping_hbm.1) | copy-start | bytes 52

commit v6 on v5

--- a/solution.py
+++ b/solution.py
@@ -93,14 +93,19 @@
     for slot, stat in enumerate(refreshed(owners)):
         block = g[stat // 2]
 
+        top, bottom = slice(0, B // 2), slice(B // 2, B)
+        quarters = [(top, top), (bottom, top) if slot == 0 else (top, bottom), (bottom, bottom)]
+
         @pl.when(stat % 2 == 0)
         def _():
-            grams[slot] = lax.dot_general(block, block, (((1,), (1,)), ((), ())), preferred_element_type=f32)
+            for r, c in quarters:
+                grams[slot, r, c] = lax.dot_general(block[r], block[c], (((1,), (1,)), ((), ())), preferred_element_type=f32)
 
         @pl.when(stat % 2 == 1)
         def _():
             flip[...] = block.T
-            grams[slot] = dot(flip[...], block)
+            for r, c in quarters:
+                grams[slot, r, c] = dot(flip[r, :], block[:, c])
 
     row = lax.broadcasted_iota(jnp.int32, (ROWS, T), 0)
     col = lax.broadcasted_iota(jnp.int32, (ROWS, T), 1)
@@ -279,20 +284,24 @@
                     keep(r, c, x, None)
                     if j >= NT // 2 and i < NT // 2:
                         keep(c, r, x.T, None)
-            if j % 2:
-                yield
+                if i % 2:
+                    yield
 
     def product(acc, a, b):
         left, right = slice(0, B // 2), slice(B // 2, B)
         acc[left, left] = dot(a[left, :], b[:, left])
         yield
-        acc[:, right] = dot(a[...], b[:, right])
+        acc[left, right] = dot(a[left, :], b[:, right])
         yield
-
-    def together(*steps):
-        steps = list(steps)
-        while steps:
-            steps = [st for st in steps if next(st, steps) is not steps]
+        acc[right, right] = dot(a[right, :], b[:, right])
+        yield
+
+    def together(work, rest):
+        for _ in work:
+            next(rest, None)
+            next(rest, None)
+        for _ in rest:
+            pass
 
     def square_off(d, ref):
         return lambda i, j, r, c: ref[r, c] * (d.cols[i] + d.rows[j])
@@ -341,9 +350,9 @@
     waiting = None
     for turn in range(16):
         work, rest = next(chains[turn % 2])
-        together(*([work] if waiting is None else [work, waiting]))
+        together(work, iter(()) if waiting is None else waiting)
         waiting = rest
-    together(waiting)
+    together(iter(()), waiting)
     lane = lax.broadcasted_iota(jnp.int32, (8, T), 1)
     line = lax.broadcasted_iota(jnp.int32, (8, T), 0)
     tail = jnp.zeros((8, T), f32)

time: 84.7 us -> 84.2 us (level)
  no operation moved by 1% of the time
where the time goes in v6:
time: 84.2 us; the launch traced here: 83.9 us
  blocking collectives  71.1 us (84%)
  Pallas kernels  12.1 us (14%)
    all_to_all x1, blocking collectives, per_device(): return graft_call(hot, lax.all_to_all(sums, COLUMN, 0, 0), update)  28.9 us
    all_to_all x1, blocking collectives, per_device(): packed = lax.all_to_all(gram_call(owners, grads), PLANE, 0, 0)  17.9 us
    all_to_all x1, blocking collectives, per_device(): packed = lax.all_to_all(sum_call(packed, CHUNKS, 'line_sum'), PLANE, 0, 0)  12.3 us
    all_to_all x1, blocking collectives, per_device(): packed = lax.all_to_all(sum_call(packed, 4, 'plane_sum'), 'z', 0, 0)  12 us
    pallas_call x1, Pallas kernels, roots_call(): pl.pallas_call(main_kernel, out_shape=[shape((NB, B, B), f32), shape((8,...  7.24 us
    pallas_call x1, Pallas kernels, gram_call(): pl.pallas_call(gram_kernel, out_shape=shape((CHUNKS, T + TAIL, T), bf16),...  2.75 us

profile of v6, /device:TPU:1, one launch (start us, length us, event | category | flops | bytes accessed | tf_op | source)
XLA Modules:
  0.0 83.9 jit_solution(14794591143081094746)
XLA Ops:
  0.0 0.0 copy-start.2
  0.0 0.7 copy-done.2
  0.7 2.8 %gram.1 = bf16[16,144,128]{2,1,0:T(8,128)(2,1)S(1)} custom-call(s32[2,2]{1,0:T(2,128)S(1)} %copy-done.2, bf16[1,2,512,512]{3,2,1,0:T(8,128)(2,1)} %g_hbm.1), custom_call_target="tpu_custom_call" | custom-call | tf_op jit(solution)/shard_map/gram/pallas_call | solution.py:395
  3.4 0.0 copy-start
  3.5 0.0 copy-start.1
  3.5 0.0 copy-start.3
  3.5 0.0 copy-start.4
  3.5 17.9 %all_to_all.20.parts = bf16[16,144,128]{2,1,0:T(8,128)(2,1)S(1)} all-to-all(bf16[16,144,128]{2,1,0:T(8,128)(2,1)S(1)} %gram.1), channel_id=1, replica_groups=mesh['z'=4,'y'=4,'x'=4,'h'=4,'c'=2] {'y','x'}, dimensions={0} | all-to-all | bytes 1179648 | tf_op jit(solution)/shard_map/all_to_all | solution.py:459
  21.4 0.6 plane_sum.1
  22.0 12.0 %all_to_all.21.parts = bf16[4,144,128]{2,1,0:T(8,128)(2,1)S(1)} all-to-all(bf16[4,144,128]{2,1,0:T(8,128)(2,1)S(1)} %plane_sum.1), channel_id=1, replica_groups=mesh['z'=4,'y'=4,'x'=4,'h'=4,'c'=2] {'z'}, dimensions={0} | all-to-all | bytes 294912 | tf_op jit(solution)/shard_map/all_to_all | solution.py:460
  34.1 0.3 line_sum.1
  34.4 12.3 %all_to_all.22.packed = bf16[16,144,128]{2,1,0:T(8,128)(2,1)S(1)} all-to-all(bf16[16,144,128]{2,1,0:T(8,128)(2,1)S(1)} %line_sum.1), channel_id=1, replica_groups=mesh['z'=4,'y'=4,'x'=4,'h'=4,'c'=2] {'y','x'}, dimensions={0} | all-to-all | bytes 1179648 | tf_op jit(solution)/shard_map/all_to_all | solution.py:461
  46.6 0.0 copy-done
  46.6 0.0 copy-done.1
  46.6 0.0 copy-done.3
  46.6 0.0 copy-done.4
  46.7 7.2 %roots_and_update.1 = (f32[2,512,512]{2,1,0:T(8,128)S(1)}, f32[8,8,128]{2,1,0:T(8,128)S(1)}, f32[8,128]{1,0:T(8,128)S(1)}) custom-call(s32[2,2]{1,0:T(2,128)S(1)} %copy-done.2, s32[2]{0:T(128)S(1)} %copy-done.3, f32[4]{0:T(128)S(1)} %copy-done.4, bf16[16,144,128]{2,1,0:T(8,128)(2,1)S(1)} %all_to_all.22.packed, bf16[2,512,512]{2,1,0:T(8,128)(2,1)S(1)} %bitcast.2, ...), custom_call_target="tpu_custom_call" | custom-call | tf_op jit(solution)/shard_map/roots_and_update/pallas_call | solution.py:419
  53.9 28.9 %all_to_all.23.sums = f32[8,8,128]{2,1,0:T(8,128)S(1)} all-to-all(f32[8,8,128]{2,1,0:T(8,128)S(1)} %get-tuple-element.9), channel_id=1, replica_groups=mesh['z'=4,'y'=4,'x'=4,'h'=4,'c'=2] {'h','c'}, dimensions={0} | all-to-all | bytes 65536 | tf_op jit(solution)/shard_map/all_to_all | solution.py:463
  82.8 1.1 %graft.1 = bf16[1,2,512,512]{3,2,1,0:T(8,128)(2,1)} custom-call(f32[8,128]{1,0:T(8,128)S(1)} %get-tuple-element.8.hot, f32[8,8,128]{2,1,0:T(8,128)S(1)} %all_to_all.23.sums, f32[2,512,512]{2,1,0:T(8,128)S(1)} %get-tuple-element.10.update), custom_call_target="tpu_custom_call" | custom-call | tf_op jit(solution)/shard_map/graft/pallas_call | solution.py:447
Async XLA Ops:
  0.0 0.7 copy-start.2
  3.4 43.2 %copy-start = (bf16[1,2,512,512]{3,2,1,0:T(8,128)(2,1)S(1)}, bf16[1,2,512,512]{3,2,1,0:T(8,128)(2,1)}, u32[]{:S(2)}) copy-start(bf16[1,2,512,512]{3,2,1,0:T(8,128)(2,1)} %g_hbm.1) | copy-start | bytes 3145732
  3.5 43.2 %copy-start.1 = (bf16[2,2,512,512]{3,2,1,0:T(8,128)(2,1)S(1)}, bf16[2,2,512,512]{3,2,1,0:T(8,128)(2,1)}, u32[]{:S(2)}) copy-start(bf16[2,2,512,512]{3,2,1,0:T(8,128)(2,1)} %param.6) | copy-start | bytes 6291460
  3.5 43.2 %copy-start.3 = (s32[2]{0:T(128)S(1)}, s32[2]{0:T(128)}, u32[]{:S(2)}) copy-start(s32[2]{0:T(128)} %layers_hbm.1) | copy-start | bytes 28
  3.5 43.2 %copy-start.4 = (f32[4]{0:T(128)S(1)}, f32[4]{0:T(128)}, u32[]{:S(2)}) copy-start(f32[4]{0:T(128)} %damping_hbm.1) | copy-start | bytes 52

commit v7 on v6

--- a/solution.py
+++ b/solution.py
@@ -150,13 +150,20 @@
 
 
 def add_parts(parts, lower):
-    total = jnp.zeros((T, T), f32)
     diag = [jnp.zeros((1, T), f32), jnp.zeros((1, T), f32)]
+    scales = []
     for p in range(parts.shape[0]):
         d, tops = read_tail(parts[p, T : T + TAIL, :])
-        total = total + decode(parts[p, :T, :], jnp.where(lower, tops[0], tops[1]))
+        scales.append(tops)
         diag = [diag[0] + d[0], diag[1] + d[1]]
-    return total, diag
+    blocks = []
+    for h in range(NT):
+        rows = slice(h * ROWS, (h + 1) * ROWS)
+        total = jnp.zeros((ROWS, T), f32)
+        for p in range(parts.shape[0]):
+            total = total + decode(parts[p, rows, :], jnp.where(lower[rows], scales[p][0], scales[p][1]))
+        blocks.append(total)
+    return jnp.concatenate(blocks, axis=0), diag
 
 
 def code_total(total, row, col):

time: 84.2 us -> 84.1 us (level)
  no operation moved by 1% of the time
where the time goes in v7:
time: 84.1 us; the launch traced here: 83.8 us
  blocking collectives  71.1 us (85%)
  Pallas kernels  12 us (14%)
    all_to_all x1, blocking collectives, per_device(): return graft_call(hot, lax.all_to_all(sums, COLUMN, 0, 0), update)  28.8 us
    all_to_all x1, blocking collectives, per_device(): packed = lax.all_to_all(gram_call(owners, grads), PLANE, 0, 0)  17.9 us
    all_to_all x1, blocking collectives, per_device(): packed = lax.all_to_all(sum_call(packed, CHUNKS, 'line_sum'), PLANE, 0, 0)  12.3 us
    all_to_all x1, blocking collectives, per_device(): packed = lax.all_to_all(sum_call(packed, 4, 'plane_sum'), 'z', 0, 0)  12.1 us
    pallas_call x1, Pallas kernels, roots_call(): pl.pallas_call(main_kernel, out_shape=[shape((NB, B, B), f32), shape((8,...  7.25 us
    pallas_call x1, Pallas kernels, gram_call(): pl.pallas_call(gram_kernel, out_shape=shape((CHUNKS, T + TAIL, T), bf16),...  2.76 us

profile of v7, /device:TPU:1, one launch (start us, length us, event | category | flops | bytes accessed | tf_op | source)
XLA Modules:
  0.0 83.8 jit_solution(6242405352594270893)
XLA Ops:
  0.0 0.0 copy-start.2
  0.0 0.7 copy-done.2
  0.7 2.8 %gram.1 = bf16[16,144,128]{2,1,0:T(8,128)(2,1)S(1)} custom-call(s32[2,2]{1,0:T(2,128)S(1)} %copy-done.2, bf16[1,2,512,512]{3,2,1,0:T(8,128)(2,1)} %g_hbm.1), custom_call_target="tpu_custom_call" | custom-call | tf_op jit(solution)/shard_map/gram/pallas_call | solution.py:402
  3.4 0.0 copy-start
  3.5 0.0 copy-start.1
  3.5 0.0 copy-start.3
  3.5 0.0 copy-start.4
  3.5 17.9 %all_to_all.20.parts = bf16[16,144,128]{2,1,0:T(8,128)(2,1)S(1)} all-to-all(bf16[16,144,128]{2,1,0:T(8,128)(2,1)S(1)} %gram.1), channel_id=1, replica_groups=mesh['z'=4,'y'=4,'x'=4,'h'=4,'c'=2] {'y','x'}, dimensions={0} | all-to-all | bytes 1179648 | tf_op jit(solution)/shard_map/all_to_all | solution.py:466
  21.4 0.6 plane_sum.1
  21.9 12.1 %all_to_all.21.parts = bf16[4,144,128]{2,1,0:T(8,128)(2,1)S(1)} all-to-all(bf16[4,144,128]{2,1,0:T(8,128)(2,1)S(1)} %plane_sum.1), channel_id=1, replica_groups=mesh['z'=4,'y'=4,'x'=4,'h'=4,'c'=2] {'z'}, dimensions={0} | all-to-all | bytes 294912 | tf_op jit(solution)/shard_map/all_to_all | solution.py:467
  34.0 0.3 line_sum.1
  34.3 12.3 %all_to_all.22.packed = bf16[16,144,128]{2,1,0:T(8,128)(2,1)S(1)} all-to-all(bf16[16,144,128]{2,1,0:T(8,128)(2,1)S(1)} %line_sum.1), channel_id=1, replica_groups=mesh['z'=4,'y'=4,'x'=4,'h'=4,'c'=2] {'y','x'}, dimensions={0} | all-to-all | bytes 1179648 | tf_op jit(solution)/shard_map/all_to_all | solution.py:468
  46.6 0.0 copy-done
  46.6 0.0 copy-done.1
  46.6 0.0 copy-done.3
  46.6 0.0 copy-done.4
  46.6 7.2 %roots_and_update.1 = (f32[2,512,512]{2,1,0:T(8,128)S(1)}, f32[8,8,128]{2,1,0:T(8,128)S(1)}, f32[8,128]{1,0:T(8,128)S(1)}) custom-call(s32[2,2]{1,0:T(2,128)S(1)} %copy-done.2, s32[2]{0:T(128)S(1)} %copy-done.3, f32[4]{0:T(128)S(1)} %copy-done.4, bf16[16,144,128]{2,1,0:T(8,128)(2,1)S(1)} %all_to_all.22.packed, bf16[2,512,512]{2,1,0:T(8,128)(2,1)S(1)} %bitcast.2, ...), custom_call_target="tpu_custom_call" | custom-call | tf_op jit(solution)/shard_map/roots_and_update/pallas_call | solution.py:426
  53.9 28.8 %all_to_all.23.sums = f32[8,8,128]{2,1,0:T(8,128)S(1)} all-to-all(f32[8,8,128]{2,1,0:T(8,128)S(1)} %get-tuple-element.9), channel_id=1, replica_groups=mesh['z'=4,'y'=4,'x'=4,'h'=4,'c'=2] {'h','c'}, dimensions={0} | all-to-all | bytes 65536 | tf_op jit(solution)/shard_map/all_to_all | solution.py:470
  82.7 1.1 %graft.1 = bf16[1,2,512,512]{3,2,1,0:T(8,128)(2,1)} custom-call(f32[8,128]{1,0:T(8,128)S(1)} %get-tuple-element.8.hot, f32[8,8,128]{2,1,0:T(8,128)S(1)} %all_to_all.23.sums, f32[2,512,512]{2,1,0:T(8,128)S(1)} %get-tuple-element.10.update), custom_call_target="tpu_custom_call" | custom-call | tf_op jit(solution)/shard_map/graft/pallas_call | solution.py:454
Async XLA Ops:
  0.0 0.7 copy-start.2
  3.4 43.1 %copy-start = (bf16[1,2,512,512]{3,2,1,0:T(8,128)(2,1)S(1)}, bf16[1,2,512,512]{3,2,1,0:T(8,128)(2,1)}, u32[]{:S(2)}) copy-start(bf16[1,2,512,512]{3,2,1,0:T(8,128)(2,1)} %g_hbm.1) | copy-start | bytes 3145732
  3.5 43.1 %copy-start.1 = (bf16[2,2,512,512]{3,2,1,0:T(8,128)(2,1)S(1)}, bf16[2,2,512,512]{3,2,1,0:T(8,128)(2,1)}, u32[]{:S(2)}) copy-start(bf16[2,2,512,512]{3,2,1,0:T(8,128)(2,1)} %param.6) | copy-start | bytes 6291460
  3.5 43.1 %copy-start.3 = (s32[2]{0:T(128)S(1)}, s32[2]{0:T(128)}, u32[]{:S(2)}) copy-start(s32[2]{0:T(128)} %layers_hbm.1) | copy-start | bytes 28
  3.5 43.1 %copy-start.4 = (f32[4]{0:T(128)S(1)}, f32[4]{0:T(128)}, u32[]{:S(2)}) copy-start(f32[4]{0:T(128)} %damping_hbm.1) | copy-start | bytes 52
